TPU v7x, 256 devices: a whole 4x4x8 slice. The times are simulated.
256 devices in a mesh: row: 32 (over z, y_lo, core), col: 8 (over x, y_hi).
Axes of the slice: x: 4, y: 4 (y_hi: 2, y_lo: 2; y = y_hi * 2 + y_lo), z: 8, core: 2. Of those that a mesh axis runs over, the one named last changes fastest.
Arguments:
- z_leaf: bfloat16 [524288, 512], P(('row', 'col')), may hold values from -6 to 6
- leaf_inverse: bfloat16 [2048, 256, 256], P(('row', 'col')), as said below
- lower_separator_coupling: bfloat16 [2048, 128, 256], P(('row', 'col')), may hold values from -0.375 to 0.375
- leaf_parent: int32 [2048], P(('row', 'col')), may hold values from 0 to 7
- leaf_offset: int32 [2048], P(('row', 'col')), may hold values from 0 to 1
- z_sep: bfloat16 [65536, 512], P(('row', 'col')), may hold values from -6 to 6
- sep_inverse: bfloat16 [256, 256, 256], P(('row', 'col')), as said below
- top_factor: bfloat16 [8, 8192, 8192], P('col', None, 'row'), may hold values from -0.09375 to 0.09375
- reader_mask: int32 [8, 32, 32], P('col', 'row'), may hold values 0 or 1
- z_top: bfloat16 [8, 8192, 512], P('col', 'row'), may hold values from -6 to 6
Outputs:
- y_leaf: bfloat16 [524288, 512], P(('row', 'col'))
- y_sep: bfloat16 [65536, 512], P(('row', 'col'))
- top_rhs: float32 [8, 8192, 512], P('col', 'row')
Inputs may be any that keep to these rules, and one draw needn't show every extreme that they name: `leaf_inverse`: each block is lower triangular with a positive diagonal. `sep_inverse`: each block is lower triangular with a positive diagonal.
All inputs are finite; a program needn't handle non-finite values. No bound on the sum of `reader_mask` on one device may be relied on, other than what follows from the above.
Results may differ from a plain program's by a relative error of at most 0.0057.
Values may be sent and summed in bfloat16 or wider, within the bound.
No kernel may reach another device: no remote copies, remote signals or barrier semaphores. Data moves between devices by JAX's collectives and lax.ppermute only.
A program may use at most 128 MiB of HBM per device.

v0:
```python
import jax
import jax.numpy as jnp
from jax import lax
from jax.sharding import PartitionSpec as P


def shards(
    z_leaf,
    leaf_inverse,
    lower_separator_coupling,
    leaf_parent,
    leaf_offset,
    z_sep,
    sep_inverse,
    top_factor,
    reader_mask,
    z_top,
):
    leaf_count = leaf_inverse.shape[0]
    panel_rows = leaf_inverse.shape[1]
    block_rows = lower_separator_coupling.shape[1]
    samples = z_sep.shape[1]
    columns = lax.axis_size("col")
    row_count = lax.axis_size("row")
    top_rows = z_top.shape[1]
    leaf_rhs = z_leaf.reshape(leaf_count, panel_rows, samples)
    solution_rows = jnp.einsum(
        "lij,ljs->lis", leaf_inverse, leaf_rhs, preferred_element_type=jnp.float32
    ).astype(jnp.bfloat16)
    panel_share = jnp.einsum(
        "qxw,qwo->qxo", lower_separator_coupling, solution_rows, preferred_element_type=jnp.float32
    )
    targets = leaf_parent * 2 + leaf_offset
    indicator_matrix = (
        targets[None, :] == jnp.arange(2 * columns, dtype=jnp.int32)[:, None]
    ).astype(jnp.float32)
    collected_rows = jnp.einsum(
        "wz,zqx->wqx", indicator_matrix, panel_share, precision=lax.Precision.HIGHEST
    )
    collected_rows = collected_rows.reshape(2 * columns * block_rows, samples)
    incoming = lax.psum_scatter(collected_rows, "col", scatter_dimension=0, tiled=True)
    reduced = (z_sep.astype(jnp.float32) - incoming).astype(jnp.bfloat16)
    sep_solved = jnp.dot(sep_inverse[0], reduced, preferred_element_type=jnp.float32).astype(
        jnp.bfloat16
    )
    readers = reader_mask[0, 0].astype(jnp.bfloat16)
    factor = top_factor[0].reshape(row_count, top_rows, panel_rows) * readers[:, None, None]
    factor_rows = factor.reshape(row_count * top_rows, panel_rows)
    summed = lax.psum_scatter(
        jnp.dot(factor_rows, sep_solved, preferred_element_type=jnp.float32),
        "row",
        scatter_dimension=0,
        tiled=True,
    )
    top_rhs = z_top[0].astype(jnp.float32) - summed
    return (solution_rows.reshape(leaf_count * panel_rows, samples), sep_solved, top_rhs[None])


def solution(mesh):
    return jax.shard_map(
        shards,
        mesh=mesh,
        in_specs=(
            P(("row", "col"), None),
            P(("row", "col"), None, None),
            P(("row", "col"), None, None),
            P(("row", "col")),
            P(("row", "col")),
            P(("row", "col"), None),
            P(("row", "col"), None, None),
            P("col", None, "row"),
            P("col", "row", None),
            P("col", "row", None),
        ),
        out_specs=(P(("row", "col"), None), P(("row", "col"), None), P("col", "row", None)),
        check_vma=False,
    )
```

profile of v0, /device:TPU:1, one launch (start us, length us, event | category | flops | bytes accessed | tf_op | source)
XLA Modules:
  0.0 326.0 jit_solution(2766844704815564528)
XLA Ops:
  7.2 0.0 copy-start
  7.2 0.0 reduce-scatter.3.cloned.1.call-start
  7.2 1.5 copy-done
  8.8 2.0 convolution_convert_fusion
  10.8 0.0 copy-start.1
  10.8 1.3 copy-done.1
  12.1 0.0 copy-done.2
  12.1 2.2 fusion.9
  14.3 3.1 copy.16
  17.4 0.0 copy-done.6
  17.4 3.5 %fusion.1 = f32[16,128,512]{2,0,1:T(8,128)S(1)} fusion(f32[8,512,128]{1,0,2:T(8,128)} %copy.16, s32[8]{0:T(128)S(1)} %multiply_add_fusion), kind=kOutput, calls=%fused_computation.2 | convolution fusion | flops 100663424 | bytes 6291488 | tf_op jit(solution)/shard_map/wz,zqx->wqx/dot_general | solution.py:37
  20.9 4.4 %copy.14 = f32[16,128,512]{2,1,0:T(8,128)} copy(f32[16,128,512]{2,0,1:T(8,128)S(1)} %fusion.1) | data formatting | bytes 8388608 | tf_op jit(solution)/shard_map/wz,zqx->wqx/dot_general | solution.py:37
  25.3 0.0 reduce-scatter.3.cloned.1.call-update
  25.3 0.0 reduce-scatter.5.cloned.1.call-start
  25.4 0.6 copy-done.8
  25.9 0.1 broadcast_bitcast_fusion
  26.0 91.9 %reduce-scatter.3.cloned.1.call-done = f32[256,512]{1,0:T(8,128)} async-done(((f32[2048,512]{1,0:T(8,128)}), f32[256,512]{1,0:T(8,128)}) %reduce-scatter.3.cloned.1.call-update) | async-done | bytes 524304 | tf_op jit(solution)/shard_map/reduce_scatter | solution.py:41
  118.0 0.0 copy-done.4
  118.0 1.3 convolution_convert_fusion.1
  119.3 8.6 %fusion = f32[8192,512]{1,0:T(8,128)} fusion(bf16[512,256]{1,0:T(8,128)(2,1)S(1)} %convolution_convert_fusion.1, bf16[1,8192,256]{2,1,0:T(8,128)(2,1)} %param.17, bf16[8192]{0:T(1024)(128)(2,1)S(1)} %bitcast.35), kind=kOutput, calls=%fused_computation.1 | convolution fusion | flops 2149580800 | bytes 21250048 | tf_op jit(solution)/shard_map/dot_general | solution.py:50
  127.9 0.0 reduce-scatter.5.cloned.1.call-update
  128.0 0.8 copy.15
  128.8 188.4 %reduce-scatter.5.cloned.1.call-done = f32[256,512]{1,0:T(8,128)} async-done(((f32[8192,512]{1,0:T(8,128)}), f32[256,512]{1,0:T(8,128)}) %reduce-scatter.5.cloned.1.call-update) | async-done | bytes 524304 | tf_op jit(solution)/shard_map/reduce_scatter | solution.py:49
  317.3 1.9 fusion.4
  (13 shorter events, 0.0 us)
Async XLA Ops:
  7.2 1.6 copy-start
  7.2 110.8 %reduce-scatter.3.cloned.1.call-start = ((), (), s32[]{:S(2)}) async-start(), calls=%async_computation.2 | async-start | bytes 4718592 | tf_op jit(solution)/shard_map/reduce_scatter | solution.py:41
  8.8 3.3 %copy-start.2 = (bf16[8,128,256]{2,1,0:T(8,128)(2,1)S(1)}, bf16[8,128,256]{2,1,0:T(8,128)(2,1)}, u32[]{:S(2)}) copy-start(bf16[8,128,256]{2,1,0:T(8,128)(2,1)} %param.12) | copy-start | bytes 1572868
  10.8 1.3 copy-start.1
  14.3 3.1 copy-start.6
  14.3 3.1 copy-start.7
  25.3 0.7 copy-start.8
  25.3 92.7 %copy-start.4 = (bf16[256,512]{1,0:T(8,128)(2,1)S(1)}, bf16[256,512]{1,0:T(8,128)(2,1)}, u32[]{:S(2)}) copy-start(bf16[256,512]{1,0:T(8,128)(2,1)} %param.15) | copy-start | bytes 786436
  25.3 92.7 %copy-start.5 = (bf16[1,256,256]{2,1,0:T(8,128)(2,1)S(1)}, bf16[1,256,256]{2,1,0:T(8,128)(2,1)}, u32[]{:S(2)}) copy-start(bf16[1,256,256]{2,1,0:T(8,128)(2,1)} %param.16) | copy-start | bytes 393220
  25.3 291.9 %reduce-scatter.5.cloned.1.call-start = ((), (), s32[]{:S(2)}) async-start(), calls=%async_computation.3 | async-start | bytes 17301504 | tf_op jit(solution)/shard_map/reduce_scatter | solution.py:49
  127.9 189.3 %copy-start.3 = (bf16[1,256,512]{2,1,0:T(8,128)(2,1)S(1)}, bf16[1,256,512]{2,1,0:T(8,128)(2,1)}, u32[]{:S(2)}) copy-start(bf16[1,256,512]{2,1,0:T(8,128)(2,1)} %param.19) | copy-start | bytes 786436
Sparse Core Ops, SparseCore 0:
  25.4 92.4 reduce-scatter.2
  128.1 189.1 reduce-scatter.4
where the time goes:
time: 326 us
  waiting for transfers between devices  280 us (86%)
  matrix products  17.6 us (5%)
  between operations  14.1 us (4%)
  local copies, waits for them, and re-layouts  11.9 us (4%)
    reduce_scatter x1, waiting for transfers between devices, shards(): lax.psum_scatter(jnp.dot(factor_rows, sep_solved, preferred_element_type=...  188 us
    reduce_scatter x1, waiting for transfers between devices, shards(): lax.psum_scatter(collected_rows, 'col', scatter_dimension=0, tiled=True)  91.9 us
    dot_general x1, matrix products, shards(): jnp.dot(factor_rows, sep_solved, preferred_element_type=jnp.float32)  8.64 us
  transfers between devices with their start and end apart: 2, of which 2 were waited for; matrix products, arithmetic and copies ran while one was open for 0% of the time, Pallas kernels for 0%

commit v1 on v0

v1 whole, which is shorter than its diff:
```python
import functools

import jax
import jax.numpy as jnp
from jax import lax
from jax.experimental import pallas as pl
from jax.experimental.pallas import tpu as pltpu
from jax.sharding import PartitionSpec as P

BF = jnp.bfloat16
F32 = jnp.float32
CHUNKS = 2
PARTS = ((0, 3), (3, 8))


def swap(x, bits):
    n = lax.axis_size("row")
    return lax.ppermute(x, "row", [(i, i ^ bits) for i in range(n)])


def chain(x):
    n = lax.axis_size("row")
    return lax.ppermute(x, "row", [(i, (i + (4 if i % 2 == 0 else n - 4)) % n) for i in range(n)])


def leaf_kernel(parent, offset, z_ref, inv_ref, coup_ref, y_ref, out_ref, acc):
    step = pl.program_id(0)

    @pl.when(step == 0)
    def _():
        acc[...] = jnp.zeros_like(acc)

    y = jnp.dot(inv_ref[0], z_ref[...], preferred_element_type=F32).astype(BF)
    y_ref[...] = y
    share = jnp.dot(coup_ref[0], y, preferred_element_type=F32)
    target = parent[step] * 2 + offset[step]
    acc[target] += share

    @pl.when(step == pl.num_programs(0) - 1)
    def _():
        out_ref[...] = acc[...].astype(BF)


def leaf_solve(z_leaf, leaf_inverse, coupling, parent, offset, targets):
    count, rows, _ = leaf_inverse.shape
    blk = coupling.shape[1]
    samples = z_leaf.shape[1]
    return pl.pallas_call(
        leaf_kernel,
        grid_spec=pltpu.PrefetchScalarGridSpec(
            num_scalar_prefetch=2,
            grid=(count,),
            in_specs=[
                pl.BlockSpec((rows, samples), lambda i, *_: (i, 0)),
                pl.BlockSpec((1, rows, rows), lambda i, *_: (i, 0, 0)),
                pl.BlockSpec((1, blk, rows), lambda i, *_: (i, 0, 0)),
            ],
            out_specs=[
                pl.BlockSpec((rows, samples), lambda i, *_: (i, 0)),
                pl.BlockSpec((targets, blk, samples), lambda i, *_: (0, 0, 0)),
            ],
            scratch_shapes=[pltpu.VMEM((targets, blk, samples), F32)],
        ),
        out_shape=[
            jax.ShapeDtypeStruct((count * rows, samples), BF),
            jax.ShapeDtypeStruct((targets, blk, samples), BF),
        ],
        compiler_params=pltpu.CompilerParams(vmem_limit_bytes=32 << 20),
        cost_estimate=pl.CostEstimate(flops=810_000_000, bytes_accessed=8 << 20, transcendentals=0),
        name="leaf_solve",
    )(parent, offset, z_leaf, leaf_inverse, coupling)


def pick_kernel(first, table, mask, *refs):
    step = pl.program_id(0)
    for m in range(4):
        keep = mask[table[m * 8 + first + step]].astype(F32)
        refs[4 + m][...] = (refs[m][...].astype(F32) * keep).astype(BF)


def pick(factor, table, mask, first, last):
    def spec(m):
        return pl.BlockSpec((256, 256), lambda i, table, mask: (table[m * 8 + first + i], 0))

    rows = (last - first) * 256
    return pl.pallas_call(
        functools.partial(pick_kernel, first),
        grid_spec=pltpu.PrefetchScalarGridSpec(
            num_scalar_prefetch=2,
            grid=(last - first,),
            in_specs=[spec(m) for m in range(4)],
            out_specs=[pl.BlockSpec((256, 256), lambda i, *_: (i, 0))] * 4,
        ),
        out_shape=[jax.ShapeDtypeStruct((rows, 256), BF)] * 4,
        compiler_params=pltpu.CompilerParams(vmem_limit_bytes=32 << 20),
        cost_estimate=pl.CostEstimate(flops=rows * 1024, bytes_accessed=rows * 4096, transcendentals=0),
        name="pick_factor",
    )(table, mask, factor, factor, factor, factor)


def sep_kernel(recv_ref, z_ref, inv_ref, y_ref):
    total = recv_ref[0].astype(F32)
    for i in range(1, recv_ref.shape[0]):
        total += recv_ref[i].astype(F32)
    reduced = (z_ref[...].astype(F32) - total).astype(BF)
    y_ref[...] = jnp.dot(inv_ref[0], reduced, preferred_element_type=F32).astype(BF)


def sep_solve(recv, z_sep, sep_inverse):
    count, rows, samples = recv.shape
    width = 128
    return pl.pallas_call(
        sep_kernel,
        grid=(samples // width,),
        in_specs=[
            pl.BlockSpec((count, rows, width), lambda i: (0, 0, i)),
            pl.BlockSpec((rows, width), lambda i: (0, i)),
            pl.BlockSpec((1, rows, rows), lambda i: (0, 0, 0)),
        ],
        out_specs=pl.BlockSpec((rows, width), lambda i: (0, i)),
        out_shape=jax.ShapeDtypeStruct((rows, samples), BF),
        compiler_params=pltpu.CompilerParams(vmem_limit_bytes=32 << 20),
        cost_estimate=pl.CostEstimate(flops=70_000_000, bytes_accessed=3 << 20, transcendentals=0),
        name="sep_solve",
    )(recv, z_sep, sep_inverse)


def stage_kernel(has_recv, add_first, final, core, *refs):
    f = refs[0:4]
    y = refs[4:8]
    total = jnp.dot(f[0][...], y[0][...], preferred_element_type=F32)
    for m in range(1, 4):
        total += jnp.dot(f[m][...], y[m][...], preferred_element_type=F32)
    if has_recv:
        recv = refs[8][...].astype(F32)
        if add_first:
            recv = jnp.where(pl.program_id(0) == core[0], recv, 0.0)
        total += recv
    if final:
        total = refs[10][...].astype(F32) - (total + refs[9][...].astype(F32))
    refs[-1][...] = total.astype(refs[-1].dtype)


def stage(core, factors, first, blocks, panels, chunk, width, recv=None, final=None):
    add_first = recv is not None and final is None and recv.shape[0] == 256
    specs = [pl.BlockSpec((256, 256), lambda i, c: (first + i, 0))] * 4
    specs += [pl.BlockSpec((256, width), lambda i, c: (0, chunk))] * 4
    args = list(factors) + list(panels)
    if recv is not None:
        if add_first:
            specs.append(pl.BlockSpec((256, width), lambda i, c: (0, 0)))
        elif final is not None:
            specs.append(pl.BlockSpec((256, width), lambda i, c: (c[0], 0)))
        else:
            specs.append(pl.BlockSpec((256, width), lambda i, c: (i, 0)))
        args.append(recv)
    dtype = BF
    if final is not None:
        other, z_top = final
        specs.append(pl.BlockSpec((256, width), lambda i, c: (0, 0)))
        specs.append(pl.BlockSpec((256, width), lambda i, c: (0, chunk)))
        args += [other, z_top]
        dtype = F32
    rows = blocks * 256
    return pl.pallas_call(
        functools.partial(stage_kernel, recv is not None, add_first, final is not None),
        grid_spec=pltpu.PrefetchScalarGridSpec(
            num_scalar_prefetch=1,
            grid=(blocks,),
            in_specs=specs,
            out_specs=pl.BlockSpec((256, width), lambda i, c: (i, 0)),
        ),
        out_shape=jax.ShapeDtypeStruct((rows, width), dtype),
        compiler_params=pltpu.CompilerParams(vmem_limit_bytes=32 << 20),
        cost_estimate=pl.CostEstimate(
            flops=rows * 2048 * width, bytes_accessed=rows * 2048 + 2048 * width, transcendentals=0
        ),
        name="stage",
    )(core, *args)


def shards(
    z_leaf,
    leaf_inverse,
    lower_separator_coupling,
    leaf_parent,
    leaf_offset,
    z_sep,
    sep_inverse,
    top_factor,
    reader_mask,
    z_top,
):
    columns = lax.axis_size("col")
    samples = z_sep.shape[1]
    me = lax.axis_index("row").astype(jnp.int32)
    core = me % 2
    table = []
    for m in range(4):
        peer = me ^ m
        sign = 1 - 2 * (peer % 2)
        base = me // 4
        pair = (peer // 2) % 2
        side = peer % 2

        def block(z, k):
            return ((z + 16) % 8) * 4 + pair * 2 + k

        table.append(block(base + 4, side))
        for d in (3, 2, 1):
            for k in (0, 1):
                table.append(block(base + d * sign, k))
        table.append(block(base, side))
    table = jnp.stack(table).astype(jnp.int32)
    mask = reader_mask[0, 0]

    y_leaf, blocks = leaf_solve(
        z_leaf, leaf_inverse, lower_separator_coupling, leaf_parent, leaf_offset, 2 * columns
    )
    sent = blocks.reshape(columns, 256, samples)
    recv = lax.all_to_all(sent, "col", split_axis=0, concat_axis=0, tiled=True)
    factors = []
    for first, last in PARTS:
        own = pick(top_factor[0], table, mask, first, last)
        factors.append([own[0]] + [swap(own[m], m) for m in (2, 3, 1)])
    factors = [[f[0], f[3], f[1], f[2]] for f in factors]
    y_sep = sep_solve(recv, z_sep, sep_inverse)
    y_pair = swap(y_sep, 2)
    y_core = swap(y_sep, 1)
    y_diag = swap(y_pair, 1)
    panels = [y_sep, y_core, y_pair, y_diag]

    core_id = core.reshape(1)
    width = samples // CHUNKS

    def where(j):
        for part, (first, last) in enumerate(PARTS):
            if first <= j < last:
                return factors[part], j - first

    held = [None] * CHUNKS
    for j, count in ((0, 1), (1, 2), (3, 2), (5, 2)):
        for c in range(CHUNKS):
            f, first = where(j)
            held[c] = chain(stage(core_id, f, first, count, panels, c, width, recv=held[c]))
    tops = []
    for c in range(CHUNKS):
        away = lax.dynamic_slice_in_dim(held[c], (1 - core) * 256, 256, axis=0)
        other = swap(away, 1)
        f, first = where(7)
        tops.append(stage(core_id, f, first, 1, panels, c, width, recv=held[c], final=(other, z_top[0])))
    top_rhs = jnp.concatenate(tops, axis=1)
    return y_leaf, y_sep, top_rhs[None]


def solution(mesh):
    return jax.shard_map(
        shards,
        mesh=mesh,
        in_specs=(
            P(("row", "col"), None),
            P(("row", "col"), None, None),
            P(("row", "col"), None, None),
            P(("row", "col")),
            P(("row", "col")),
            P(("row", "col"), None),
            P(("row", "col"), None, None),
            P("col", None, "row"),
            P("col", "row", None),
            P("col", "row", None),
        ),
        out_specs=(P(("row", "col"), None), P(("row", "col"), None), P("col", "row", None)),
        check_vma=False,
    )
```

time: 326 us -> 130 us (0.40)
  waiting for transfers between devices: 280 us -> 46.6 us
  starting transfers between devices: 0.08 us -> 41.3 us
  Pallas kernels: 0 us -> 22.4 us
  matrix products: 17.6 us -> 0 us
  between operations: 14.1 us -> 0.81 us
  local copies, waits for them, and re-layouts: 11.9 us -> 17.4 us
    reduce_scatter x2 -> x0, waiting for transfers between devices: 280 us -> none  [the longest x1 188 us: shards(): lax.psum_scatter(jnp.dot(factor_rows, sep_solved, preferred_element_type=...]
    ppermute x0 -> x19, starting transfers between devices: none -> 33.6 us  [the longest x8 21.2 us: chain(): lax.ppermute(x, 'row', [(i, (i + (4 if i % 2 == 0 else n - 4)) % n) for i...]
    all_to_all x0 -> x1, waiting for transfers between devices: none -> 23.5 us  [shards(): recv = lax.all_to_all(sent, 'col', split_axis=0, concat_axis=0, tiled=True)]
    ppermute x0 -> x19, waiting for transfers between devices: none -> 23 us  [the longest x11 20.3 us: swap(): return lax.ppermute(x, 'row', [(i, i ^ bits) for i in range(n)])]
    pallas_call x0 -> x14, Pallas kernels: none -> 22.4 us  [the longest x10 11.1 us: stage(): pl.pallas_call(functools.partial(stage_kernel, recv is not None, add_firs...]
    dot_general x5 -> x0, matrix products: 17.6 us -> none  [the longest x1 8.64 us: shards(): jnp.dot(factor_rows, sep_solved, preferred_element_type=jnp.float32)]
    unnamed x21 -> x38, local copies, waits for them, and re-layouts: 4.39 us -> 16.4 us
    all_to_all x0 -> x1, starting transfers between devices: none -> 7.61 us  [shards(): recv = lax.all_to_all(sent, 'col', split_axis=0, concat_axis=0, tiled=True)]
  transfers between devices with their start and end apart: 2 -> 20, of which waited for: 2 -> 6; matrix products, arithmetic and copies ran while one was open for 0% -> 1% of each run, Pallas kernels for 0% -> 13%
where the time goes in v1:
time: 130 us; the launch traced here: 129 us
  waiting for transfers between devices  46.6 us (36%)
  starting transfers between devices  41.3 us (32%)
  Pallas kernels  22.4 us (17%)
  local copies, waits for them, and re-layouts  17.4 us (13%)
    all_to_all x1, waiting for transfers between devices, shards(): recv = lax.all_to_all(sent, 'col', split_axis=0, concat_axis=0, tiled=True)  23.5 us
    ppermute x8, starting transfers between devices, chain(): lax.ppermute(x, 'row', [(i, (i + (4 if i % 2 == 0 else n - 4)) % n) for i...  21.2 us
    ppermute x11, waiting for transfers between devices, swap(): return lax.ppermute(x, 'row', [(i, i ^ bits) for i in range(n)])  20.3 us
    unnamed x38, local copies, waits for them, and re-layouts  16.4 us
    ppermute x11, starting transfers between devices, swap(): return lax.ppermute(x, 'row', [(i, i ^ bits) for i in range(n)])  12.4 us
    pallas_call x10, Pallas kernels, stage(): pl.pallas_call(functools.partial(stage_kernel, recv is not None, add_firs...  11.1 us
    all_to_all x1, starting transfers between devices, shards(): recv = lax.all_to_all(sent, 'col', split_axis=0, concat_axis=0, tiled=True)  7.61 us
    pallas_call x1, Pallas kernels, leaf_solve(): pl.pallas_call(leaf_kernel, grid_spec=pltpu.PrefetchScalarGridSpec(num_sc...  5.8 us
  transfers between devices with their start and end apart: 20, of which 6 were waited for; matrix products, arithmetic and copies ran while one was open for 1% of the time, Pallas kernels for 13%

profile of v1, /device:TPU:1, one launch (start us, length us, event | category | flops | bytes accessed | tf_op | source)
XLA Modules:
  0.0 129.3 jit_solution(17995117626380956770)
XLA Ops:
  0.6 1.6 %copy-done.9 = bf16[2048,512]{1,0:T(8,128)(2,1)S(1)} copy-done((bf16[2048,512]{1,0:T(8,128)(2,1)S(1)}, bf16[2048,512]{1,0:T(8,128)(2,1)}, u32[]{:S(2)}) %copy-start.9) | copy-done | bytes 2097176
  5.8 5.8 %leaf_solve.1 = (bf16[2048,512]{1,0:T(8,128)(2,1)}, bf16[16,128,512]{2,1,0:T(8,128)(2,1)S(1)}) custom-call(s32[8]{0:T(128)S(1)} %copy-done.17, s32[8]{0:T(128)S(1)} %copy-done.18, bf16[2048,512]{1,0:T(8,128)(2,1)S(1)} %copy-done.9, bf16[8,256,256]{2,1,0:T(8,128)(2,1)S(1)} %copy-done.12, bf16[8,128,256]{2,1,0:T(8,128)(2,1)S(1)} %copy-done.13), custom_call_target="tpu_custom_call" | custom-call | flops 810000000 | bytes 8388608 | tf_op jit(solution)/shard_map/leaf_solve/pallas_call | solution.py:48
  11.6 1.4 %copy-done.10 = bf16[16,128,512]{2,1,0:T(8,128)(2,1)} copy-done((bf16[16,128,512]{2,1,0:T(8,128)(2,1)}, bf16[16,128,512]{2,1,0:T(8,128)(2,1)S(1)}, u32[]{:S(2)}) %copy-start.10) | copy-done | bytes 2097176
  13.0 7.6 %all-to-all-start = ((bf16[8,256,512]{2,1,0:T(8,128)(2,1)}), bf16[8,256,512]{2,1,0:T(8,128)(2,1)S(1)}, u32[]{:S(2)}, u32[]{:S(2)}) async-start(bf16[8,256,512]{2,1,0:T(8,128)(2,1)} %bitcast.47), calls=%async_computation | async-start | bytes 4194304 | tf_op jit(solution)/shard_map/all_to_all | solution.py:221
  20.7 2.2 %copy-done = bf16[1,8192,256]{2,1,0:T(8,128)(2,1)S(1)} copy-done((bf16[1,8192,256]{2,1,0:T(8,128)(2,1)S(1)}, bf16[1,8192,256]{2,1,0:T(8,128)(2,1)}, u32[]{:S(2)}) %copy-start) | copy-done | bytes 4194328
  22.9 2.1 %pick_factor.3 = (bf16[768,256]{1,0:T(8,128)(2,1)S(1)}, bf16[768,256]{1,0:T(8,128)(2,1)}, bf16[768,256]{1,0:T(8,128)(2,1)}, bf16[768,256]{1,0:T(8,128)(2,1)}) custom-call(s32[32]{0:T(128)S(1)} %stack.131.table, s32[32]{0:T(128)S(1)} %bitcast.50, bf16[8192,256]{1,0:T(8,128)(2,1)S(1)} %bitcast.39, bf16[8192,256]{1,0:T(8,128)(2,1)S(1)} %bitcast.40, ...), custom_call_target="tpu_custom_call" | custom-call | flops 786432 | bytes 3145728 | tf_op jit(solution)/shard_map/pick_factor/pallas_call | solution.py:86
  27.6 23.5 %all-to-all-done.recv_ref = bf16[8,256,512]{2,1,0:T(8,128)(2,1)S(1)} async-done(((bf16[8,256,512]{2,1,0:T(8,128)(2,1)}), bf16[8,256,512]{2,1,0:T(8,128)(2,1)S(1)}, u32[]{:S(2)}, u32[]{:S(2)}) %all-to-all-start) | async-done | bytes 2097184 | tf_op jit(solution)/shard_map/all_to_all | solution.py:221
  52.1 2.3 %sep_solve.1.refs_4_ = bf16[256,512]{1,0:T(8,128)(2,1)} custom-call(bf16[8,256,512]{2,1,0:T(8,128)(2,1)S(1)} %all-to-all-done.recv_ref, bf16[256,512]{1,0:T(8,128)(2,1)S(1)} %copy-done.14, bf16[1,256,256]{2,1,0:T(8,128)(2,1)S(1)} %copy-done.15), custom_call_target="tpu_custom_call" | custom-call | flops 70000000 | bytes 3145728 | tf_op jit(solution)/shard_map/sep_solve/pallas_call | solution.py:112
  54.8 1.9 %collective-permute-start.3 = (bf16[256,512]{1,0:T(8,128)(2,1)}, bf16[256,512]{1,0:T(8,128)(2,1)S(1)}, u32[]{:S(2)}, u32[]{:S(2)}) collective-permute-start(bf16[256,512]{1,0:T(8,128)(2,1)} %sep_solve.1.refs_4_), channel_id=1, source_target_pairs={{0,8},{8,0},{16,24},{24,16},{32,40},{40,32},{48,56},{56,48},{64,72... | collective-permute-start | bytes 786440 | tf_op jit(solution)/shard_map/ppermute | solution.py:18
  56.7 9.5 %collective-permute-done.4.refs_6_ = bf16[256,512]{1,0:T(8,128)(2,1)S(1)} collective-permute-done((bf16[256,512]{1,0:T(8,128)(2,1)}, bf16[256,512]{1,0:T(8,128)(2,1)S(1)}, u32[]{:S(2)}, u32[]{:S(2)}) %collective-permute-start.4) | collective-permute-done | bytes 262176 | tf_op jit(solution)/shard_map/ppermute | solution.py:18
  66.2 1.5 %collective-permute-start.5 = (bf16[256,512]{1,0:T(8,128)(2,1)S(1)}, bf16[256,512]{1,0:T(8,128)(2,1)S(1)}, u32[]{:S(2)}, u32[]{:S(2)}) collective-permute-start(bf16[256,512]{1,0:T(8,128)(2,1)S(1)} %collective-permute-done.4.refs_6_), channel_id=1, source_target_pairs={{0,8},{8,0},{16,24},{24,16},{32,40},{40,32},{48,56},{56,48},{64,72... | collective-permute-start | bytes 786440 | tf_op jit(solution)/shard_map/ppermute | solution.py:18
  67.8 2.2 %copy-done.1 = bf16[1,8192,256]{2,1,0:T(8,128)(2,1)S(1)} copy-done((bf16[1,8192,256]{2,1,0:T(8,128)(2,1)S(1)}, bf16[1,8192,256]{2,1,0:T(8,128)(2,1)}, u32[]{:S(2)}) %copy-start.1) | copy-done | bytes 4194328
  77.9 5.7 %collective-permute-start.14 = (bf16[256,256]{1,0:T(8,128)(2,1)S(1)}, bf16[256,256]{1,0:T(8,128)(2,1)S(1)}, u32[]{:S(2)}, u32[]{:S(2)}) collective-permute-start(bf16[256,256]{1,0:T(8,128)(2,1)S(1)} %stage.15), channel_id=1, source_target_pairs={{0,32},{8,232},{16,48},{24,248},{32,64},{40,8},{48,80},{56,24},{64... | collective-permute-start | bytes 393224 | tf_op jit(solution)/shard_map/ppermute | solution.py:23
  85.6 1.6 %stage.16 = bf16[512,256]{1,0:T(8,128)(2,1)S(1)} custom-call(s32[1]{0:T(128)} %bitcast.1.core, bf16[768,256]{1,0:T(8,128)(2,1)S(1)} %get-tuple-element.19.refs_0_, bf16[768,256]{1,0:T(8,128)(2,1)S(1)} %copy-done.6, bf16[768,256]{1,0:T(8,128)(2,1)S(1)} %copy-done.8, bf16[768,256]{1,0:T(8,128)(2,1)} %collective-permute-done.8.refs_3_, ...), custom_call_target="tpu_custom_call" | custom-call | flops 268435456 | bytes 1572864 | tf_op jit(solution)/shard_map/stage/pallas_call | solution.py:165
  87.2 3.1 %collective-permute-start.15 = (bf16[512,256]{1,0:T(8,128)(2,1)S(1)}, bf16[512,256]{1,0:T(8,128)(2,1)S(1)}, u32[]{:S(2)}, u32[]{:S(2)}) collective-permute-start(bf16[512,256]{1,0:T(8,128)(2,1)S(1)} %stage.16), channel_id=1, source_target_pairs={{0,32},{8,232},{16,48},{24,248},{32,64},{40,8},{48,80},{56,24},{64... | collective-permute-start | bytes 786440 | tf_op jit(solution)/shard_map/ppermute | solution.py:23
  90.2 1.6 %stage.11 = bf16[512,256]{1,0:T(8,128)(2,1)S(1)} custom-call(s32[1]{0:T(128)} %bitcast.1.core, bf16[768,256]{1,0:T(8,128)(2,1)S(1)} %get-tuple-element.19.refs_0_, bf16[768,256]{1,0:T(8,128)(2,1)S(1)} %copy-done.6, bf16[768,256]{1,0:T(8,128)(2,1)S(1)} %copy-done.8, bf16[768,256]{1,0:T(8,128)(2,1)} %collective-permute-done.8.refs_3_, ...), custom_call_target="tpu_custom_call" | custom-call | flops 268435456 | bytes 1572864 | tf_op jit(solution)/shard_map/stage/pallas_call | solution.py:165
  92.3 10.8 %collective-permute-done.2.refs_3_ = bf16[1280,256]{1,0:T(8,128)(2,1)S(1)} collective-permute-done((bf16[1280,256]{1,0:T(8,128)(2,1)S(1)}, bf16[1280,256]{1,0:T(8,128)(2,1)S(1)}, u32[]{:S(2)}, u32[]{:S(2)}) %collective-permute-start.2) | collective-permute-done | bytes 655392 | tf_op jit(solution)/shard_map/ppermute | solution.py:18
  103.7 5.7 %collective-permute-start.16 = (bf16[512,256]{1,0:T(8,128)(2,1)S(1)}, bf16[512,256]{1,0:T(8,128)(2,1)S(1)}, u32[]{:S(2)}, u32[]{:S(2)}) collective-permute-start(bf16[512,256]{1,0:T(8,128)(2,1)S(1)} %stage.17), channel_id=1, source_target_pairs={{0,32},{8,232},{16,48},{24,248},{32,64},{40,8},{48,80},{56,24},{64... | collective-permute-start | bytes 786440 | tf_op jit(solution)/shard_map/ppermute | solution.py:23
  111.1 1.6 %collective-permute-done.16.refs_8_ = bf16[512,256]{1,0:T(8,128)(2,1)S(1)} collective-permute-done((bf16[512,256]{1,0:T(8,128)(2,1)S(1)}, bf16[512,256]{1,0:T(8,128)(2,1)S(1)}, u32[]{:S(2)}, u32[]{:S(2)}) %collective-permute-start.16) | collective-permute-done | bytes 262176 | tf_op jit(solution)/shard_map/ppermute | solution.py:23
  112.7 1.3 %stage.18 = bf16[512,256]{1,0:T(8,128)(2,1)} custom-call(s32[1]{0:T(128)} %bitcast.1.core, bf16[1280,256]{1,0:T(8,128)(2,1)S(1)} %get-tuple-element.15.refs_0_, bf16[1280,256]{1,0:T(8,128)(2,1)S(1)} %collective-permute-done.refs_1_, bf16[1280,256]{1,0:T(8,128)(2,1)S(1)} %collective-permute-done.1.refs_2_, ...), custom_call_target="tpu_custom_call" | custom-call | flops 268435456 | bytes 1572864 | tf_op jit(solution)/shard_map/stage/pallas_call | solution.py:165
  114.0 3.1 %collective-permute-start.17 = (bf16[512,256]{1,0:T(8,128)(2,1)}, bf16[512,256]{1,0:T(8,128)(2,1)}, u32[]{:S(2)}, u32[]{:S(2)}) collective-permute-start(bf16[512,256]{1,0:T(8,128)(2,1)} %stage.18), channel_id=1, source_target_pairs={{0,32},{8,232},{16,48},{24,248},{32,64},{40,8},{48,80},{56,24},{64... | collective-permute-start | bytes 786440 | tf_op jit(solution)/shard_map/ppermute | solution.py:23
  118.5 1.5 %collective-permute-start.12 = (bf16[512,256]{1,0:T(8,128)(2,1)}, bf16[512,256]{1,0:T(8,128)(2,1)S(1)}, u32[]{:S(2)}, u32[]{:S(2)}) collective-permute-start(bf16[512,256]{1,0:T(8,128)(2,1)} %stage.13), channel_id=1, source_target_pairs={{0,32},{8,232},{16,48},{24,248},{32,64},{40,8},{48,80},{56,24},{64... | collective-permute-start | bytes 786440 | tf_op jit(solution)/shard_map/ppermute | solution.py:23
  121.7 2.3 %collective-permute-start.18 = (bf16[256,256]{1,0:T(8,128)(2,1)S(1)}, bf16[256,256]{1,0:T(8,128)(2,1)S(1)}, u32[]{:S(2)}, u32[]{:S(2)}) collective-permute-start(bf16[256,256]{1,0:T(8,128)(2,1)S(1)} %constant_dynamic-slice_fusion), channel_id=1, source_target_pairs={{0,8},{8,0},{16,24},{24,16},{32,40},{40,32},{48,56},{56,48},{64,72... | collective-permute-start | bytes 393224 | tf_op jit(solution)/shard_map/ppermute | solution.py:18
  124.2 1.6 %collective-permute-start.13 = (bf16[256,256]{1,0:T(8,128)(2,1)S(1)}, bf16[256,256]{1,0:T(8,128)(2,1)S(1)}, u32[]{:S(2)}, u32[]{:S(2)}) collective-permute-start(bf16[256,256]{1,0:T(8,128)(2,1)S(1)} %constant_dynamic-slice_fusion.1), channel_id=1, source_target_pairs={{0,8},{8,0},{16,24},{24,16},{32,40},{40,32},{48,56},{56,48},{64,72... | collective-permute-start | bytes 393224 | tf_op jit(solution)/shard_map/ppermute | solution.py:18
  (72 shorter events, 27.2 us)
Async XLA Ops:
  13.0 7.7 %copy-start.16 = (s32[1,1,32]{2,1,0:T(1,128)S(1)}, s32[1,1,32]{2,1,0:T(1,128)}, u32[]{:S(2)}) copy-start(s32[1,1,32]{2,1,0:T(1,128)} %param.18) | copy-start | bytes 388
  13.0 38.1 %all-to-all-start = ((bf16[8,256,512]{2,1,0:T(8,128)(2,1)}), bf16[8,256,512]{2,1,0:T(8,128)(2,1)S(1)}, u32[]{:S(2)}, u32[]{:S(2)}) async-start(bf16[8,256,512]{2,1,0:T(8,128)(2,1)} %bitcast.47), calls=%async_computation | async-start | bytes 4194304 | tf_op jit(solution)/shard_map/all_to_all | solution.py:221
  22.9 28.2 %copy-start.15 = (bf16[1,256,256]{2,1,0:T(8,128)(2,1)S(1)}, bf16[1,256,256]{2,1,0:T(8,128)(2,1)}, u32[]{:S(2)}) copy-start(bf16[1,256,256]{2,1,0:T(8,128)(2,1)} %inv_ref.3) | copy-start | bytes 393220
  25.0 46.0 %collective-permute-start.6 = (bf16[768,256]{1,0:T(8,128)(2,1)}, bf16[768,256]{1,0:T(8,128)(2,1)S(1)}, u32[]{:S(2)}, u32[]{:S(2)}) collective-permute-start(bf16[768,256]{1,0:T(8,128)(2,1)} %get-tuple-element.20), channel_id=1, source_target_pairs={{0,8},{8,0},{16,24},{24,16},{32,40},{40,32},{48,56},{56,48},{64,72... | collective-permute-start | bytes 1179656 | tf_op jit(solution)/shard_map/ppermute | solution.py:18
  25.9 45.9 %collective-permute-start.7 = (bf16[768,256]{1,0:T(8,128)(2,1)}, bf16[768,256]{1,0:T(8,128)(2,1)S(1)}, u32[]{:S(2)}, u32[]{:S(2)}) collective-permute-start(bf16[768,256]{1,0:T(8,128)(2,1)} %get-tuple-element.21), channel_id=1, source_target_pairs={{0,16},{8,24},{16,0},{24,8},{32,48},{40,56},{48,32},{56,40},{64,80... | collective-permute-start | bytes 1179656 | tf_op jit(solution)/shard_map/ppermute | solution.py:18
  26.3 47.3 %collective-permute-start.8 = (bf16[768,256]{1,0:T(8,128)(2,1)}, bf16[768,256]{1,0:T(8,128)(2,1)}, u32[]{:S(2)}, u32[]{:S(2)}) collective-permute-start(bf16[768,256]{1,0:T(8,128)(2,1)} %get-tuple-element.22), channel_id=1, source_target_pairs={{0,24},{8,16},{16,8},{24,0},{32,56},{40,48},{48,40},{56,32},{64,88... | collective-permute-start | bytes 1179656 | tf_op jit(solution)/shard_map/ppermute | solution.py:18
  54.4 11.9 %collective-permute-start.4 = (bf16[256,512]{1,0:T(8,128)(2,1)}, bf16[256,512]{1,0:T(8,128)(2,1)S(1)}, u32[]{:S(2)}, u32[]{:S(2)}) collective-permute-start(bf16[256,512]{1,0:T(8,128)(2,1)} %sep_solve.1.refs_4_), channel_id=1, source_target_pairs={{0,16},{8,24},{16,0},{24,8},{32,48},{40,56},{48,32},{56,40},{64,80... | collective-permute-start | bytes 786440 | tf_op jit(solution)/shard_map/ppermute | solution.py:18
  54.8 19.9 %collective-permute-start.3 = (bf16[256,512]{1,0:T(8,128)(2,1)}, bf16[256,512]{1,0:T(8,128)(2,1)S(1)}, u32[]{:S(2)}, u32[]{:S(2)}) collective-permute-start(bf16[256,512]{1,0:T(8,128)(2,1)} %sep_solve.1.refs_4_), channel_id=1, source_target_pairs={{0,8},{8,0},{16,24},{24,16},{32,40},{40,32},{48,56},{56,48},{64,72... | collective-permute-start | bytes 786440 | tf_op jit(solution)/shard_map/ppermute | solution.py:18
  66.2 8.5 %collective-permute-start.5 = (bf16[256,512]{1,0:T(8,128)(2,1)S(1)}, bf16[256,512]{1,0:T(8,128)(2,1)S(1)}, u32[]{:S(2)}, u32[]{:S(2)}) collective-permute-start(bf16[256,512]{1,0:T(8,128)(2,1)S(1)} %collective-permute-done.4.refs_6_), channel_id=1, source_target_pairs={{0,8},{8,0},{16,24},{24,16},{32,40},{40,32},{48,56},{56,48},{64,72... | collective-permute-start | bytes 786440 | tf_op jit(solution)/shard_map/ppermute | solution.py:18
  71.8 20.5 %collective-permute-start = (bf16[1280,256]{1,0:T(8,128)(2,1)S(1)}, bf16[1280,256]{1,0:T(8,128)(2,1)S(1)}, u32[]{:S(2)}, u32[]{:S(2)}) collective-permute-start(bf16[1280,256]{1,0:T(8,128)(2,1)S(1)} %get-tuple-element.16), channel_id=1, source_target_pairs={{0,8},{8,0},{16,24},{24,16},{32,40},{40,32},{48,56},{56,48},{64,72... | collective-permute-start | bytes 1966088 | tf_op jit(solution)/shard_map/ppermute | solution.py:18
  72.5 19.7 %collective-permute-start.1 = (bf16[1280,256]{1,0:T(8,128)(2,1)S(1)}, bf16[1280,256]{1,0:T(8,128)(2,1)S(1)}, u32[]{:S(2)}, u32[]{:S(2)}) collective-permute-start(bf16[1280,256]{1,0:T(8,128)(2,1)S(1)} %get-tuple-element.17), channel_id=1, source_target_pairs={{0,16},{8,24},{16,0},{24,8},{32,48},{40,56},{48,32},{56,40},{64,80... | collective-permute-start | bytes 1966088 | tf_op jit(solution)/shard_map/ppermute | solution.py:18
  73.6 29.4 %collective-permute-start.2 = (bf16[1280,256]{1,0:T(8,128)(2,1)S(1)}, bf16[1280,256]{1,0:T(8,128)(2,1)S(1)}, u32[]{:S(2)}, u32[]{:S(2)}) collective-permute-start(bf16[1280,256]{1,0:T(8,128)(2,1)S(1)} %get-tuple-element.18), channel_id=1, source_target_pairs={{0,24},{8,16},{16,8},{24,0},{32,56},{40,48},{48,40},{56,32},{64,88... | collective-permute-start | bytes 1966088 | tf_op jit(solution)/shard_map/ppermute | solution.py:18
  77.9 7.7 %collective-permute-start.14 = (bf16[256,256]{1,0:T(8,128)(2,1)S(1)}, bf16[256,256]{1,0:T(8,128)(2,1)S(1)}, u32[]{:S(2)}, u32[]{:S(2)}) collective-permute-start(bf16[256,256]{1,0:T(8,128)(2,1)S(1)} %stage.15), channel_id=1, source_target_pairs={{0,32},{8,232},{16,48},{24,248},{32,64},{40,8},{48,80},{56,24},{64... | collective-permute-start | bytes 393224 | tf_op jit(solution)/shard_map/ppermute | solution.py:23
  84.8 5.5 %collective-permute-start.9 = (bf16[256,256]{1,0:T(8,128)(2,1)S(1)}, bf16[256,256]{1,0:T(8,128)(2,1)S(1)}, u32[]{:S(2)}, u32[]{:S(2)}) collective-permute-start(bf16[256,256]{1,0:T(8,128)(2,1)S(1)} %stage.10), channel_id=1, source_target_pairs={{0,32},{8,232},{16,48},{24,248},{32,64},{40,8},{48,80},{56,24},{64... | collective-permute-start | bytes 393224 | tf_op jit(solution)/shard_map/ppermute | solution.py:23
  87.2 15.9 %collective-permute-start.15 = (bf16[512,256]{1,0:T(8,128)(2,1)S(1)}, bf16[512,256]{1,0:T(8,128)(2,1)S(1)}, u32[]{:S(2)}, u32[]{:S(2)}) collective-permute-start(bf16[512,256]{1,0:T(8,128)(2,1)S(1)} %stage.16), channel_id=1, source_target_pairs={{0,32},{8,232},{16,48},{24,248},{32,64},{40,8},{48,80},{56,24},{64... | collective-permute-start | bytes 786440 | tf_op jit(solution)/shard_map/ppermute | solution.py:23
  91.8 17.6 %collective-permute-start.10 = (bf16[512,256]{1,0:T(8,128)(2,1)S(1)}, bf16[512,256]{1,0:T(8,128)(2,1)S(1)}, u32[]{:S(2)}, u32[]{:S(2)}) collective-permute-start(bf16[512,256]{1,0:T(8,128)(2,1)S(1)} %stage.11), channel_id=1, source_target_pairs={{0,32},{8,232},{16,48},{24,248},{32,64},{40,8},{48,80},{56,24},{64... | collective-permute-start | bytes 786440 | tf_op jit(solution)/shard_map/ppermute | solution.py:23
  103.1 14.1 %copy-start.3 = (bf16[1280,256]{1,0:T(8,128)(2,1)}, bf16[1280,256]{1,0:T(8,128)(2,1)S(1)}, u32[]{:S(2)}) copy-start(bf16[1280,256]{1,0:T(8,128)(2,1)S(1)} %collective-permute-done.2.refs_3_) | copy-start | bytes 1966084
  103.7 9.0 %collective-permute-start.16 = (bf16[512,256]{1,0:T(8,128)(2,1)S(1)}, bf16[512,256]{1,0:T(8,128)(2,1)S(1)}, u32[]{:S(2)}, u32[]{:S(2)}) collective-permute-start(bf16[512,256]{1,0:T(8,128)(2,1)S(1)} %stage.17), channel_id=1, source_target_pairs={{0,32},{8,232},{16,48},{24,248},{32,64},{40,8},{48,80},{56,24},{64... | collective-permute-start | bytes 786440 | tf_op jit(solution)/shard_map/ppermute | solution.py:23
  110.1 7.1 %collective-permute-start.11 = (bf16[512,256]{1,0:T(8,128)(2,1)S(1)}, bf16[512,256]{1,0:T(8,128)(2,1)S(1)}, u32[]{:S(2)}, u32[]{:S(2)}) collective-permute-start(bf16[512,256]{1,0:T(8,128)(2,1)S(1)} %stage.12), channel_id=1, source_target_pairs={{0,32},{8,232},{16,48},{24,248},{32,64},{40,8},{48,80},{56,24},{64... | collective-permute-start | bytes 786440 | tf_op jit(solution)/shard_map/ppermute | solution.py:23
  114.0 11.8 %copy-start.11 = (bf16[1,256,512]{2,1,0:T(8,128)(2,1)S(1)}, bf16[1,256,512]{2,1,0:T(8,128)(2,1)}, u32[]{:S(2)}) copy-start(bf16[1,256,512]{2,1,0:T(8,128)(2,1)} %param.19) | copy-start | bytes 786436
  114.0 6.7 %collective-permute-start.17 = (bf16[512,256]{1,0:T(8,128)(2,1)}, bf16[512,256]{1,0:T(8,128)(2,1)}, u32[]{:S(2)}, u32[]{:S(2)}) collective-permute-start(bf16[512,256]{1,0:T(8,128)(2,1)} %stage.18), channel_id=1, source_target_pairs={{0,32},{8,232},{16,48},{24,248},{32,64},{40,8},{48,80},{56,24},{64... | collective-permute-start | bytes 786440 | tf_op jit(solution)/shard_map/ppermute | solution.py:23
  118.5 5.7 %collective-permute-start.12 = (bf16[512,256]{1,0:T(8,128)(2,1)}, bf16[512,256]{1,0:T(8,128)(2,1)S(1)}, u32[]{:S(2)}, u32[]{:S(2)}) collective-permute-start(bf16[512,256]{1,0:T(8,128)(2,1)} %stage.13), channel_id=1, source_target_pairs={{0,32},{8,232},{16,48},{24,248},{32,64},{40,8},{48,80},{56,24},{64... | collective-permute-start | bytes 786440 | tf_op jit(solution)/shard_map/ppermute | solution.py:23
  121.7 4.1 %collective-permute-start.18 = (bf16[256,256]{1,0:T(8,128)(2,1)S(1)}, bf16[256,256]{1,0:T(8,128)(2,1)S(1)}, u32[]{:S(2)}, u32[]{:S(2)}) collective-permute-start(bf16[256,256]{1,0:T(8,128)(2,1)S(1)} %constant_dynamic-slice_fusion), channel_id=1, source_target_pairs={{0,8},{8,0},{16,24},{24,16},{32,40},{40,32},{48,56},{56,48},{64,72... | collective-permute-start | bytes 393224 | tf_op jit(solution)/shard_map/ppermute | solution.py:18
  124.2 3.9 %collective-permute-start.13 = (bf16[256,256]{1,0:T(8,128)(2,1)S(1)}, bf16[256,256]{1,0:T(8,128)(2,1)S(1)}, u32[]{:S(2)}, u32[]{:S(2)}) collective-permute-start(bf16[256,256]{1,0:T(8,128)(2,1)S(1)} %constant_dynamic-slice_fusion.1), channel_id=1, source_target_pairs={{0,8},{8,0},{16,24},{24,16},{32,40},{40,32},{48,56},{56,48},{64,72... | collective-permute-start | bytes 393224 | tf_op jit(solution)/shard_map/ppermute | solution.py:18
  (15 other events, 21.2 us)

commit v2 on v0

v2 whole, which is shorter than its diff:
```python
import functools

import jax
import jax.numpy as jnp
from jax import lax
from jax.experimental import pallas as pl
from jax.experimental.pallas import tpu as pltpu
from jax.sharding import PartitionSpec as P

BF = jnp.bfloat16
F32 = jnp.float32
CHUNKS = 2
SPLIT = 5


def swap(x, bits):
    n = lax.axis_size("row")
    return lax.ppermute(x, "row", [(i, i ^ bits) for i in range(n)])


def chain(x, chips=1, cross=0):
    n = lax.axis_size("row")
    hop = 4 * chips
    return lax.ppermute(
        x, "row", [(i, ((i + (hop if i % 2 == 0 else n - hop)) % n) ^ cross) for i in range(n)]
    )


def across(x, step, cross=0):
    n = lax.axis_size("col")
    return lax.ppermute(x, "col", [(i, ((i + 2 * step) % n) ^ cross) for i in range(n)])


def diagonal(x):
    rows, cols = lax.axis_size("row"), lax.axis_size("col")
    return lax.ppermute(
        x, ("row", "col"), [(r * cols + c, (r ^ 2) * cols + (c ^ 1)) for r in range(rows) for c in range(cols)]
    )


def leaf_kernel(place, parent, offset, z_ref, inv_ref, coup_ref, y_ref, *refs):
    up2, down2, up0, up1, down0, down1, own, z, inv, coup, y, acc, in_sem, out_sem = refs
    count = inv.shape[0]
    reads, writes = [], []
    for i in range(count):
        rows = pl.ds(i * 256, 256)
        reads.append(
            [
                pltpu.make_async_copy(inv_ref.at[i], inv.at[i], in_sem.at[3 * i]),
                pltpu.make_async_copy(z_ref.at[rows, :], z.at[rows, :], in_sem.at[3 * i + 1]),
                pltpu.make_async_copy(coup_ref.at[i], coup.at[i], in_sem.at[3 * i + 2]),
            ]
        )
        for copy in reads[i]:
            copy.start()
    acc[...] = jnp.zeros_like(acc)
    for i in range(count):
        for copy in reads[i]:
            copy.wait()
        rows = slice(i * 256, i * 256 + 256)
        solved = jnp.dot(inv[i], z[rows, :], preferred_element_type=F32).astype(BF)
        y[rows, :] = solved
        writes.append(
            pltpu.make_async_copy(
                y.at[pl.ds(i * 256, 256), :], y_ref.at[pl.ds(i * 256, 256), :], out_sem.at[i]
            )
        )
        writes[i].start()
        p = parent[i]
        away = ((p >> 1) - place[1]) & 3
        side = (p & 1) ^ place[2]
        acc[(away * 2 + offset[i]) * 2 + side] += jnp.dot(coup[i], solved, preferred_element_type=F32)
    up2[...] = acc[8:10].astype(BF)
    down2[...] = acc[10:12].astype(BF)
    own[...] = acc[0:4]
    up0[...] = acc[4:6].astype(BF)
    up1[...] = acc[6:8].astype(BF)
    down0[...] = acc[12:14].astype(BF)
    down1[...] = acc[14:16].astype(BF)
    for copy in writes:
        copy.wait()


def leaf_solve(place, z_leaf, leaf_inverse, coupling, parent, offset, targets):
    count, rows, _ = leaf_inverse.shape
    blk = coupling.shape[1]
    samples = z_leaf.shape[1]
    return pl.pallas_call(
        leaf_kernel,
        grid_spec=pltpu.PrefetchScalarGridSpec(
            num_scalar_prefetch=3,
            grid=(1,),
            in_specs=[pl.BlockSpec(memory_space=pl.ANY)] * 3,
            out_specs=[pl.BlockSpec(memory_space=pl.ANY)]
            + [pl.BlockSpec((2, blk, samples), lambda i, *_: (0, 0, 0))] * 6
            + [pl.BlockSpec((4, blk, samples), lambda i, *_: (0, 0, 0))],
            scratch_shapes=[
                pltpu.VMEM(z_leaf.shape, BF),
                pltpu.VMEM(leaf_inverse.shape, BF),
                pltpu.VMEM(coupling.shape, BF),
                pltpu.VMEM(z_leaf.shape, BF),
                pltpu.VMEM((targets, blk, samples), F32),
                pltpu.SemaphoreType.DMA((3 * count,)),
                pltpu.SemaphoreType.DMA((count,)),
            ],
        ),
        out_shape=[jax.ShapeDtypeStruct((count * rows, samples), BF)]
        + [jax.ShapeDtypeStruct((2, blk, samples), BF)] * 6
        + [jax.ShapeDtypeStruct((4, blk, samples), F32)],
        compiler_params=pltpu.CompilerParams(vmem_limit_bytes=24 << 20),
        cost_estimate=pl.CostEstimate(flops=810_000_000, bytes_accessed=8 << 20, transcendentals=0),
        name="leaf_solve",
    )(place, parent, offset, z_leaf, leaf_inverse, coupling)


def gather_kernel(own, from0, from1, back0, back1, z_ref, part_ref, mine_ref, rest_ref):
    for b, (f, g) in enumerate(((from0, back0), (from1, back1))):
        rows = slice(b * 128, b * 128 + 128)
        rest = z_ref[rows, :].astype(F32) - (own[2 * b] + f[0].astype(F32) + g[0].astype(F32))
        rest_ref[rows, :] = rest
        mine_ref[rows, :] = rest.astype(BF)
        part_ref[rows, :] = (own[2 * b + 1] + f[1].astype(F32) + g[1].astype(F32)).astype(BF)


def gather_x(own, from0, from1, back0, back1, z_sep):
    shape = z_sep.shape
    return pl.pallas_call(
        gather_kernel,
        out_shape=[
            jax.ShapeDtypeStruct(shape, BF),
            jax.ShapeDtypeStruct(shape, BF),
            jax.ShapeDtypeStruct(shape, F32),
        ],
        compiler_params=pltpu.CompilerParams(vmem_limit_bytes=16 << 20),
        cost_estimate=pl.CostEstimate(flops=2_000_000, bytes_accessed=4 << 20, transcendentals=0),
        name="gather_x",
    )(own, from0, from1, back0, back1, z_sep)


def block_of(me, m, j):
    peer = me ^ m
    z, pair, side = peer >> 2, (peer >> 1) & 1, peer & 1
    sign = 1 - 2 * side
    if j == 0:
        z, side = z + 4, side
    elif j < 7:
        z, side = z + sign * (3 - (j - 1) // 2), (j - 1) % 2
    return ((z + 8) & 7) * 4 + pair * 2 + side


def pick_kernel(wanted, place, mask, factor, extra, *refs):
    outs = refs[: len(wanted)]
    held, in_sem, out_sem = refs[len(wanted) :]
    jobs = []
    for o, groups in enumerate(wanted):
        order = [(m, j) for m, lo, hi in groups for j in range(lo, hi)]
        jobs += [(o, m, j, at) for at, (m, j) in enumerate(order)]
    reads, writes = [], []
    for i, (o, m, j, at) in enumerate(jobs):
        block = pl.multiple_of(block_of(place[0], m, j) * 256, 256)
        reads.append(pltpu.make_async_copy(factor.at[pl.ds(block, 256), :], held.at[i], in_sem.at[i]))
        reads[-1].start()
    if extra is not None:
        tail = outs[-1].shape[0] - 256
        reads.append(pltpu.make_async_copy(extra, held.at[len(jobs)], in_sem.at[len(jobs)]))
        reads[-1].start()
    for i, (o, m, j, at) in enumerate(jobs):
        reads[i].wait()
        keep = mask[block_of(place[0], m, j)].astype(F32)
        held[i] = (held[i].astype(F32) * keep).astype(BF)
        writes.append(
            pltpu.make_async_copy(held.at[i], outs[o].at[pl.ds(at * 256, 256), :], out_sem.at[i])
        )
        writes[-1].start()
    if extra is not None:
        reads[-1].wait()
        writes.append(
            pltpu.make_async_copy(held.at[len(jobs)], outs[-1].at[pl.ds(tail, 256), :], out_sem.at[len(jobs)])
        )
        writes[-1].start()
    for copy in writes:
        copy.wait()


def pick(place, mask, factor, wanted, limit, extra=None):
    sizes = [sum(hi - lo for _, lo, hi in groups) for groups in wanted]
    total = sum(sizes)
    kernel = functools.partial(pick_kernel, wanted)
    args = [factor]
    if extra is None:
        kernel = lambda place, mask, factor, *refs: pick_kernel(wanted, place, mask, factor, None, *refs)
    else:
        sizes[-1] += 1
        args.append(extra)
    return pl.pallas_call(
        kernel,
        grid_spec=pltpu.PrefetchScalarGridSpec(
            num_scalar_prefetch=2,
            grid=(1,),
            in_specs=[pl.BlockSpec(memory_space=pl.ANY)] * len(args),
            out_specs=[pl.BlockSpec(memory_space=pl.ANY)] * len(wanted),
            scratch_shapes=[
                pltpu.VMEM((total + 1, 256, 256), BF),
                pltpu.SemaphoreType.DMA((total + 1,)),
                pltpu.SemaphoreType.DMA((total + 1,)),
            ],
        ),
        out_shape=[jax.ShapeDtypeStruct((size * 256, 256), BF) for size in sizes],
        compiler_params=pltpu.CompilerParams(vmem_limit_bytes=limit),
        cost_estimate=pl.CostEstimate(flops=total << 16, bytes_accessed=total << 18, transcendentals=0),
        name="pick_factor",
    )(place, mask, *args)


def sep_kernel(rest_ref, part_ref, near_ref, cross_ref, inv_ref, near_inv_ref, y_ref, pair_ref):
    mine = (rest_ref[...] - part_ref[...].astype(F32)).astype(BF)
    y = jnp.dot(inv_ref[0], mine, preferred_element_type=F32).astype(BF)
    y_ref[...] = y
    near = (near_ref[...].astype(F32) - cross_ref[...].astype(F32)).astype(BF)
    pair_ref[0:256, :] = y
    pair_ref[256:512, :] = jnp.dot(near_inv_ref[...], near, preferred_element_type=F32).astype(BF)


def sep_solve(rest, part, near, cross, sep_inverse, far_f):
    rows, samples = rest.shape
    whole = pl.BlockSpec((rows, samples), lambda i: (0, 0))
    last = far_f.shape[0] // rows - 1
    return pl.pallas_call(
        sep_kernel,
        grid=(1,),
        in_specs=[whole] * 4
        + [
            pl.BlockSpec((1, rows, rows), lambda i: (0, 0, 0)),
            pl.BlockSpec((rows, rows), lambda i: (last, 0)),
        ],
        out_specs=[whole, pl.BlockSpec((2 * rows, samples), lambda i: (0, 0))],
        out_shape=[
            jax.ShapeDtypeStruct((rows, samples), BF),
            jax.ShapeDtypeStruct((2 * rows, samples), BF),
        ],
        compiler_params=pltpu.CompilerParams(vmem_limit_bytes=16 << 20),
        cost_estimate=pl.CostEstimate(flops=140_000_000, bytes_accessed=2 << 20, transcendentals=0),
        name="sep_solve",
    )(rest, part, near, cross, sep_inverse, far_f)


def multiply(f, y):
    total = jnp.dot(f[0][...], y[0][...], preferred_element_type=F32)
    for m in range(1, 4):
        total += jnp.dot(f[m][...], y[m][...], preferred_element_type=F32)
    return total


def start_kernel(*refs):
    refs[8][...] = multiply(refs[0:4], refs[4:8]).astype(BF)


def start(factors, first, blocks, panels, chunk, width):
    return pl.pallas_call(
        start_kernel,
        grid=(blocks,),
        in_specs=[pl.BlockSpec((256, 256), lambda i: (first + i, 0))] * 4
        + [pl.BlockSpec((256, width), lambda i, m=m: (m // 2, chunk)) for m in range(4)],
        out_specs=pl.BlockSpec((256, width), lambda i: (i, 0)),
        out_shape=jax.ShapeDtypeStruct((256 * blocks, width), BF),
        compiler_params=pltpu.CompilerParams(vmem_limit_bytes=16 << 20),
        cost_estimate=pl.CostEstimate(flops=blocks * 512 * 1024 * width, bytes_accessed=3 << 20, transcendentals=0),
        name="chain_start",
    )(*factors, *panels)


def middle_kernel(core, *refs):
    total = multiply(refs[0:4], refs[4:8]) + refs[8][...].astype(F32)
    total += jnp.where(pl.program_id(0) == core[0], refs[9][...].astype(F32), 0.0)
    refs[10][...] = total.astype(BF)


def middle(core, factors, first, panels, chunk, width, near, far):
    return pl.pallas_call(
        middle_kernel,
        grid_spec=pltpu.PrefetchScalarGridSpec(
            num_scalar_prefetch=1,
            grid=(2,),
            in_specs=[pl.BlockSpec((256, 256), lambda i, c: (first + i, 0))] * 4
            + [pl.BlockSpec((256, width), lambda i, c, m=m: (m // 2, chunk)) for m in range(4)]
            + [
                pl.BlockSpec((256, width), lambda i, c: (i, 0)),
                pl.BlockSpec((256, width), lambda i, c: (0, chunk)),
            ],
            out_specs=pl.BlockSpec((256, width), lambda i, c: (i, 0)),
        ),
        out_shape=jax.ShapeDtypeStruct((512, width), BF),
        compiler_params=pltpu.CompilerParams(vmem_limit_bytes=16 << 20),
        cost_estimate=pl.CostEstimate(flops=1024 * 1024 * width, bytes_accessed=3 << 20, transcendentals=0),
        name="chain_middle",
    )(core, *factors, *panels, near, far)


def last_kernel(core, *refs):
    total = (multiply(refs[0:4], refs[4:8]) + refs[8][...].astype(F32)).astype(BF)

    @pl.when(pl.program_id(0) == 0)
    def _():
        refs[9][...] = total

    @pl.when(pl.program_id(0) == 1)
    def _():
        refs[10][...] = total


def last(core, factors, first, panels, chunk, width, recv):
    return pl.pallas_call(
        last_kernel,
        grid_spec=pltpu.PrefetchScalarGridSpec(
            num_scalar_prefetch=1,
            grid=(2,),
            in_specs=[pl.BlockSpec((256, 256), lambda i, c, k=k: (k + (c[0] ^ i), 0)) for k in first]
            + [pl.BlockSpec((256, width), lambda i, c, m=m: (m // 2, chunk)) for m in range(4)]
            + [pl.BlockSpec((256, width), lambda i, c: (c[0] ^ i, 0))],
            out_specs=[pl.BlockSpec((256, width), lambda i, c: (0, 0))] * 2,
        ),
        out_shape=[jax.ShapeDtypeStruct((256, width), BF)] * 2,
        compiler_params=pltpu.CompilerParams(vmem_limit_bytes=16 << 20),
        cost_estimate=pl.CostEstimate(flops=1024 * 1024 * width, bytes_accessed=3 << 20, transcendentals=0),
        name="chain_last",
    )(core, *factors, *panels, recv)


def own_kernel(*refs):
    refs[9][...] = refs[8][...].astype(F32) - multiply(refs[0:4], refs[4:8])


def own_rows(factors, first, panels, z_top):
    samples = z_top.shape[1]
    return pl.pallas_call(
        own_kernel,
        grid=(1,),
        in_specs=[pl.BlockSpec((256, 256), lambda i, k=k: (k, 0)) for k in first]
        + [pl.BlockSpec((256, samples), lambda i, m=m: (m // 2, 0)) for m in range(4)]
        + [pl.BlockSpec((256, samples), lambda i: (0, 0))],
        out_specs=pl.BlockSpec((256, samples), lambda i: (0, 0)),
        out_shape=jax.ShapeDtypeStruct((256, samples), F32),
        compiler_params=pltpu.CompilerParams(vmem_limit_bytes=16 << 20),
        cost_estimate=pl.CostEstimate(flops=512 * 1024 * samples, bytes_accessed=3 << 20, transcendentals=0),
        name="own_rows",
    )(*factors, *panels, z_top)


def shards(
    z_leaf,
    leaf_inverse,
    lower_separator_coupling,
    leaf_parent,
    leaf_offset,
    z_sep,
    sep_inverse,
    top_factor,
    reader_mask,
    z_top,
):
    columns = lax.axis_size("col")
    samples = z_sep.shape[1]
    me = lax.axis_index("row").astype(jnp.int32)
    col = lax.axis_index("col").astype(jnp.int32)
    core = me & 1
    place = jnp.stack([me, col >> 1, col & 1])
    mask = reader_mask[0, 0]

    near_f, far_a = pick(
        place, mask, top_factor[0], (((1, 0, 8),), ((2, 0, SPLIT), (3, 0, SPLIT))), 60 << 20, sep_inverse[0]
    )
    far_a = swap(far_a, 2)
    z_leaf, near_f = lax.optimization_barrier((z_leaf, near_f))
    near_f = swap(near_f, 1)
    y_leaf, up2, down2, up0, up1, down0, down1, own = leaf_solve(
        place, z_leaf, leaf_inverse, lower_separator_coupling, leaf_parent, leaf_offset, 2 * columns
    )
    from2, back2 = across(up2, 1), across(down2, 3)
    from1, back0 = across(up1, 1), across(down0, 3)
    own_f, far_b, cross_b = pick(
        place, mask, top_factor[0], (((0, 0, 8),), ((2, SPLIT, 8),), ((3, SPLIT, 8),)), 16 << 20)
    from1, near_f, far_a, own_f, far_b, cross_b = lax.optimization_barrier(
        (from1, near_f, far_a, own_f, far_b, cross_b)
    )
    cross_a = swap(far_a[SPLIT * 256 : 2 * SPLIT * 256], 1)
    near_inverse = far_a[2 * SPLIT * 256 :]
    from0 = across((up0.astype(F32) + from2.astype(F32)).astype(BF), 1)
    back1 = across((down1.astype(F32) + back2.astype(F32)).astype(BF), 3)
    part, mine, rest = gather_x(own, from0, from1, back0, back1, z_sep)
    theirs, cross, near = across(part, 0, 1), diagonal(part), swap(mine, 2)
    y_sep, pair = sep_solve(rest, theirs, near, cross, sep_inverse, near_inverse)
    pair_core = swap(pair, 1)
    pair_core, far_b, cross_b = lax.optimization_barrier((pair_core, far_b, cross_b))
    far_b, cross_b = swap(far_b, 2), swap(cross_b, 3)
    panels = [pair, pair_core, pair, pair_core]
    first_f = [own_f, near_f, far_a, cross_a]
    skip = (SPLIT, SPLIT, 0, 0)

    core_id = core.reshape(1)
    width = samples // CHUNKS
    far = chain(start(first_f, 0, 1, panels, 0, samples), 2)
    arrived = [chain(start(first_f, 1, 2, panels, c, width)) for c in range(CHUNKS)]
    sums = [middle(core_id, first_f, 3, panels, c, width, arrived[c], far) for c in range(CHUNKS)]
    last_f = [own_f, near_f, far_b, cross_b]
    arrived = [chain(x) for x in sums]
    for c in range(CHUNKS):
        same, other = last(core_id, last_f, skip, panels, c, width, arrived[c])
        arrived[c] = (chain(same), chain(other, 1, 1))
    rest = own_rows(last_f, [k + 2 for k in skip], panels, z_top[0])
    tops = [
        rest[:, c * width : (c + 1) * width] - (arrived[c][0].astype(F32) + arrived[c][1].astype(F32))
        for c in range(CHUNKS)
    ]
    top_rhs = jnp.concatenate(tops, axis=1)
    return y_leaf, y_sep, top_rhs[None]


def solution(mesh):
    return jax.shard_map(
        shards,
        mesh=mesh,
        in_specs=(
            P(("row", "col"), None),
            P(("row", "col"), None, None),
            P(("row", "col"), None, None),
            P(("row", "col")),
            P(("row", "col")),
            P(("row", "col"), None),
            P(("row", "col"), None, None),
            P("col", None, "row"),
            P("col", "row", None),
            P("col", "row", None),
        ),
        out_specs=(P(("row", "col"), None), P(("row", "col"), None), P("col", "row", None)),
        check_vma=False,
    )
```

time: 326 us -> 103 us (0.32)
  waiting for transfers between devices: 280 us -> 29.7 us
  starting transfers between devices: 0.08 us -> 36.7 us
  Pallas kernels: 0 us -> 29.2 us
  matrix products: 17.6 us -> 0 us
  between operations: 14.1 us -> 0.92 us
  local copies, waits for them, and re-layouts: 11.9 us -> 4.17 us
    reduce_scatter x2 -> x0, waiting for transfers between devices: 280 us -> none  [the longest x1 188 us: shards(): lax.psum_scatter(jnp.dot(factor_rows, sep_solved, preferred_element_type=...]
    ppermute x0 -> x24, starting transfers between devices: none -> 36.7 us  [the longest x9 16.1 us: chain(): lax.ppermute(x, 'row', [(i, (i + (hop if i % 2 == 0 else n - hop)) % n ^...]
    ppermute x0 -> x24, waiting for transfers between devices: none -> 29.7 us  [the longest x7 16.3 us: across(): lax.ppermute(x, 'col', [(i, (i + 2 * step) % n ^ cross) for i in range(n)])]
    pallas_call x0 -> x13, Pallas kernels: none -> 29.2 us  [the longest x2 9.41 us: pick(): pl.pallas_call(kernel, grid_spec=pltpu.PrefetchScalarGridSpec(num_scalar_...]
    dot_general x5 -> x0, matrix products: 17.6 us -> none  [the longest x1 8.64 us: shards(): jnp.dot(factor_rows, sep_solved, preferred_element_type=jnp.float32)]
    dot_general x2 -> x0, local copies, waits for them, and re-layouts: 7.49 us -> none  [the longest x1 4.38 us: shards(): jnp.einsum('wz,zqx->wqx', indicator_matrix, panel_share, precision=lax.Pr...]
  transfers between devices with their start and end apart: 2 -> 24, of which waited for: 2 -> 9; matrix products, arithmetic and copies ran while one was open for 0% -> 0% of each run, Pallas kernels for 0% -> 23%
where the time goes in v2:
time: 103 us; the launch traced here: 102 us
  starting transfers between devices  36.7 us (36%)
  waiting for transfers between devices  29.7 us (29%)
  Pallas kernels  29.2 us (28%)
  local copies, waits for them, and re-layouts  4.17 us (4%)
  other arithmetic  1.65 us (2%)
    ppermute x7, waiting for transfers between devices, across(): lax.ppermute(x, 'col', [(i, (i + 2 * step) % n ^ cross) for i in range(n)])  16.3 us
    ppermute x9, starting transfers between devices, chain(): lax.ppermute(x, 'row', [(i, (i + (hop if i % 2 == 0 else n - hop)) % n ^...  16.1 us
    ppermute x7, starting transfers between devices, swap(): return lax.ppermute(x, 'row', [(i, i ^ bits) for i in range(n)])  11.9 us
    pallas_call x2, Pallas kernels, pick(): pl.pallas_call(kernel, grid_spec=pltpu.PrefetchScalarGridSpec(num_scalar_...  9.41 us
    ppermute x7, waiting for transfers between devices, swap(): return lax.ppermute(x, 'row', [(i, i ^ bits) for i in range(n)])  7.97 us
    pallas_call x1, Pallas kernels, leaf_solve(): pl.pallas_call(leaf_kernel, grid_spec=pltpu.PrefetchScalarGridSpec(num_sc...  6.99 us
    ppermute x7, starting transfers between devices, across(): lax.ppermute(x, 'col', [(i, (i + 2 * step) % n ^ cross) for i in range(n)])  6.41 us
    ppermute x9, waiting for transfers between devices, chain(): lax.ppermute(x, 'row', [(i, (i + (hop if i % 2 == 0 else n - hop)) % n ^...  4.24 us
  transfers between devices with their start and end apart: 24, of which 9 were waited for; matrix products, arithmetic and copies ran while one was open for 0% of the time, Pallas kernels for 23%

profile of v2, /device:TPU:1, one launch (start us, length us, event | category | flops | bytes accessed | tf_op | source)
XLA Modules:
  0.0 102.3 jit_solution(1319264341003657327)
XLA Ops:
  1.2 3.7 %pick_factor.2 = (bf16[2048,256]{1,0:T(8,128)(2,1)}, bf16[2816,256]{1,0:T(8,128)(2,1)}) custom-call(s32[3]{0:T(128)} %pad_add_fusion.place, s32[32]{0:T(128)} %bitcast.14, bf16[8192,256]{1,0:T(8,128)(2,1)} %bitcast.10, bf16[256,256]{1,0:T(8,128)(2,1)} %bitcast.12), custom_call_target="tpu_custom_call" | custom-call | flops 1179648 | bytes 4718592 | tf_op jit(solution)/shard_map/pick_factor/pallas_call | solution.py:195
  4.9 2.2 %collective-permute-start.4 = (bf16[2816,256]{1,0:T(8,128)(2,1)}, bf16[2816,256]{1,0:T(8,128)(2,1)S(1)}, u32[]{:S(2)}, u32[]{:S(2)}) collective-permute-start(bf16[2816,256]{1,0:T(8,128)(2,1)} %get-tuple-element.44), channel_id=1, source_target_pairs={{0,16},{8,24},{16,0},{24,8},{32,48},{40,56},{48,32},{56,40},{64,80... | collective-permute-start | bytes 4325384 | tf_op jit(solution)/shard_map/ppermute | solution.py:18
  8.4 1.6 %copy-done.5 = bf16[2048,512]{1,0:T(8,128)(2,1)S(1)} copy-done((bf16[2048,512]{1,0:T(8,128)(2,1)S(1)}, bf16[2048,512]{1,0:T(8,128)(2,1)}, u32[]{:S(2)}) %copy-start.5) | copy-done | bytes 2097176
  10.0 7.0 %leaf_solve.1 = (bf16[2048,512]{1,0:T(8,128)(2,1)}, bf16[2,128,512]{2,1,0:T(8,128)(2,1)S(1)}, bf16[2,128,512]{2,1,0:T(8,128)(2,1)S(1)}, bf16[2,128,512]{2,1,0:T(...) custom-call(s32[3]{0:T(128)S(1)} %copy-done.11, ...), custom_call_target="tpu_custom_call" | custom-call | flops 810000000 | bytes 8388608 | tf_op jit(solution)/shard_map/leaf_solve/pallas_call | solution.py:88
  19.8 6.3 %collective-permute-done = bf16[2,128,512]{2,1,0:T(8,128)(2,1)S(1)} collective-permute-done((bf16[2,128,512]{2,1,0:T(8,128)(2,1)S(1)}, bf16[2,128,512]{2,1,0:T(8,128)(2,1)S(1)}, u32[]{:S(2)}, u32[]{:S(2)}) %collective-permute-start) | collective-permute-done | bytes 262176 | tf_op jit(solution)/shard_map/ppermute | solution.py:31
  26.0 1.5 %collective-permute-start.5 = (bf16[2,128,512]{2,1,0:T(8,128)(2,1)S(1)}, bf16[2,128,512]{2,1,0:T(8,128)(2,1)S(1)}, u32[]{:S(2)}, u32[]{:S(2)}) collective-permute-start(bf16[2,128,512]{2,1,0:T(8,128)(2,1)S(1)} %get-tuple-element.49), channel_id=1, source_target_pairs={{0,6},{1,7},{2,0},{3,1},{4,2},{5,3},{6,4},{7,5},{8,14},{9,15},{10,... | collective-permute-start | bytes 786440 | tf_op jit(solution)/shard_map/ppermute | solution.py:31
  27.8 3.8 %collective-permute-done.2.from1 = bf16[2,128,512]{2,1,0:T(8,128)(2,1)S(1)} collective-permute-done((bf16[2,128,512]{2,1,0:T(8,128)(2,1)S(1)}, bf16[2,128,512]{2,1,0:T(8,128)(2,1)S(1)}, u32[]{:S(2)}, u32[]{:S(2)}) %collective-permute-start.2) | collective-permute-done | bytes 262176 | tf_op jit(solution)/shard_map/ppermute | solution.py:31
  31.7 1.5 %collective-permute-start.7 = (bf16[2,128,512]{2,1,0:T(8,128)(2,1)S(1)}, bf16[2,128,512]{2,1,0:T(8,128)(2,1)S(1)}, u32[]{:S(2)}, u32[]{:S(2)}) collective-permute-start(bf16[2,128,512]{2,1,0:T(8,128)(2,1)S(1)} %add_convert_fusion), channel_id=1, source_target_pairs={{0,6},{1,7},{2,0},{3,1},{4,2},{5,3},{6,4},{7,5},{8,14},{9,15},{10,... | collective-permute-start | bytes 786440 | tf_op jit(solution)/shard_map/ppermute | solution.py:31
  33.2 5.8 %pick_factor.3 = (bf16[2048,256]{1,0:T(8,128)(2,1)S(1)}, bf16[768,256]{1,0:T(8,128)(2,1)}, bf16[768,256]{1,0:T(8,128)(2,1)}) custom-call(s32[3]{0:T(128)S(1)} %copy-done.11, s32[32]{0:T(128)S(1)} %bitcast.15, bf16[8192,256]{1,0:T(8,128)(2,1)S(1)} %bitcast.11), custom_call_target="tpu_custom_call" | custom-call | flops 917504 | bytes 3670016 | tf_op jit(solution)/shard_map/pick_factor/pallas_call | solution.py:195
  39.9 2.3 %collective-permute-start.10 = (bf16[256,512]{1,0:T(8,128)(2,1)S(1)}, bf16[256,512]{1,0:T(8,128)(2,1)S(1)}, u32[]{:S(2)}, u32[]{:S(2)}) collective-permute-start(bf16[256,512]{1,0:T(8,128)(2,1)S(1)} %get-tuple-element.53), channel_id=1, source_target_pairs={{0,17},{1,16},{2,19},{3,18},{4,21},{5,20},{6,23},{7,22},{8,25},{9,... | collective-permute-start | bytes 786440 | tf_op jit(solution)/shard_map/ppermute | solution.py:36
  42.8 2.4 %collective-permute-start.14 = (bf16[1280,256]{1,0:T(8,128)(2,1)S(1)}, bf16[1280,256]{1,0:T(8,128)(2,1)S(1)}, u32[]{:S(2)}, u32[]{:S(2)}) collective-permute-start(bf16[1280,256]{1,0:T(8,128)(2,1)S(1)} %slice.14), channel_id=1, source_target_pairs={{0,8},{8,0},{16,24},{24,16},{32,40},{40,32},{48,56},{56,48},{64,72... | collective-permute-start | bytes 1966088 | tf_op jit(solution)/shard_map/ppermute | solution.py:18
  47.0 6.2 %collective-permute-done.8.part_ref = bf16[256,512]{1,0:T(8,128)(2,1)S(1)} collective-permute-done((bf16[256,512]{1,0:T(8,128)(2,1)S(1)}, bf16[256,512]{1,0:T(8,128)(2,1)S(1)}, u32[]{:S(2)}, u32[]{:S(2)}) %collective-permute-start.8) | collective-permute-done | bytes 262176 | tf_op jit(solution)/shard_map/ppermute | solution.py:31
  54.2 2.6 %collective-permute-start.11 = (bf16[512,512]{1,0:T(8,128)(2,1)S(1)}, bf16[512,512]{1,0:T(8,128)(2,1)S(1)}, u32[]{:S(2)}, u32[]{:S(2)}) collective-permute-start(bf16[512,512]{1,0:T(8,128)(2,1)S(1)} %get-tuple-element.59.refs_4_.refs_6_), channel_id=1, source_target_pairs={{0,8},{8,0},{16,24},{24,16},{32,40},{40,32},{48,56},{56,48},{64,72... | collective-permute-start | bytes 1572872 | tf_op jit(solution)/shard_map/ppermute | solution.py:18
  59.6 5.5 %collective-permute-start.15 = (bf16[512,256]{1,0:T(8,128)(2,1)}, bf16[512,256]{1,0:T(8,128)(2,1)}, u32[]{:S(2)}, u32[]{:S(2)}) collective-permute-start(bf16[512,256]{1,0:T(8,128)(2,1)} %chain_start.3), channel_id=1, source_target_pairs={{0,32},{8,232},{16,48},{24,248},{32,64},{40,8},{48,80},{56,24},{64... | collective-permute-start | bytes 786440 | tf_op jit(solution)/shard_map/ppermute | solution.py:24
  69.5 2.8 %collective-permute-start.13 = (bf16[768,256]{1,0:T(8,128)(2,1)}, bf16[768,256]{1,0:T(8,128)(2,1)}, u32[]{:S(2)}, u32[]{:S(2)}) collective-permute-start(bf16[768,256]{1,0:T(8,128)(2,1)} %get-tuple-element.63), channel_id=1, source_target_pairs={{0,24},{8,16},{16,8},{24,0},{32,56},{40,48},{48,40},{56,32},{64,88... | collective-permute-start | bytes 1179656 | tf_op jit(solution)/shard_map/ppermute | solution.py:18
  76.3 1.6 %chain_middle.2 = bf16[512,256]{1,0:T(8,128)(2,1)S(1)} custom-call(s32[1]{0:T(128)} %bitcast.7.core, bf16[2048,256]{1,0:T(8,128)(2,1)S(1)} %get-tuple-element.57.refs_0_, bf16[2048,256]{1,0:T(8,128)(2,1)S(1)} %collective-permute-done.3.refs_1_, bf16[2816,256]{1,0:T(8,128)(2,1)S(1)} %copy-done.1, bf16[1280,256]{1,0:T(8,128)(2,1)S(1)} %copy-done.4, ...), custom_call_target="tpu_custom_call" | custom-call | flops 268435456 | bytes 3145728 | tf_op jit(solution)/shard_map/chain_middle/pallas_call | solution.py:279
  78.0 3.7 %collective-permute-start.17 = (bf16[512,256]{1,0:T(8,128)(2,1)S(1)}, bf16[512,256]{1,0:T(8,128)(2,1)S(1)}, u32[]{:S(2)}, u32[]{:S(2)}) collective-permute-start(bf16[512,256]{1,0:T(8,128)(2,1)S(1)} %chain_middle.2), channel_id=1, source_target_pairs={{0,32},{8,232},{16,48},{24,248},{32,64},{40,8},{48,80},{56,24},{64... | collective-permute-start | bytes 786440 | tf_op jit(solution)/shard_map/ppermute | solution.py:24
  81.7 1.6 %chain_middle.3 = bf16[512,256]{1,0:T(8,128)(2,1)S(1)} custom-call(s32[1]{0:T(128)} %bitcast.7.core, bf16[2048,256]{1,0:T(8,128)(2,1)S(1)} %get-tuple-element.57.refs_0_, bf16[2048,256]{1,0:T(8,128)(2,1)S(1)} %collective-permute-done.3.refs_1_, bf16[2816,256]{1,0:T(8,128)(2,1)S(1)} %copy-done.1, bf16[1280,256]{1,0:T(8,128)(2,1)S(1)} %copy-done.4, ...), custom_call_target="tpu_custom_call" | custom-call | flops 268435456 | bytes 3145728 | tf_op jit(solution)/shard_map/chain_middle/pallas_call | solution.py:279
  83.5 5.8 %collective-permute-done.13.refs_3_ = bf16[768,256]{1,0:T(8,128)(2,1)} collective-permute-done((bf16[768,256]{1,0:T(8,128)(2,1)}, bf16[768,256]{1,0:T(8,128)(2,1)}, u32[]{:S(2)}, u32[]{:S(2)}) %collective-permute-start.13) | collective-permute-done | bytes 393248 | tf_op jit(solution)/shard_map/ppermute | solution.py:18
  89.3 1.6 %chain_last.2 = (bf16[256,256]{1,0:T(8,128)(2,1)S(1)}, bf16[256,256]{1,0:T(8,128)(2,1)S(1)}) custom-call(s32[1]{0:T(128)} %bitcast.7.core, bf16[2048,256]{1,0:T(8,128)(2,1)S(1)} %get-tuple-element.57.refs_0_, bf16[2048,256]{1,0:T(8,128)(2,1)S(1)} %collective-permute-done.3.refs_1_, bf16[768,256]{1,0:T(8,128)(2,1)S(1)} %collective-permute-done.12.refs_2_, ...), custom_call_target="tpu_custom_call" | custom-call | flops 268435456 | bytes 3145728 | tf_op jit(solution)/shard_map/chain_last/pallas_call | solution.py:312
  91.0 1.6 %collective-permute-start.19 = (bf16[256,256]{1,0:T(8,128)(2,1)S(1)}, bf16[256,256]{1,0:T(8,128)(2,1)S(1)}, u32[]{:S(2)}, u32[]{:S(2)}) collective-permute-start(bf16[256,256]{1,0:T(8,128)(2,1)S(1)} %get-tuple-element.66), channel_id=1, source_target_pairs={{0,40},{8,224},{16,56},{24,240},{32,72},{40,0},{48,88},{56,16},{64... | collective-permute-start | bytes 393224 | tf_op jit(solution)/shard_map/ppermute | solution.py:24
  92.5 1.6 %chain_last.3 = (bf16[256,256]{1,0:T(8,128)(2,1)S(1)}, bf16[256,256]{1,0:T(8,128)(2,1)S(1)}) custom-call(s32[1]{0:T(128)} %bitcast.7.core, bf16[2048,256]{1,0:T(8,128)(2,1)S(1)} %get-tuple-element.57.refs_0_, bf16[2048,256]{1,0:T(8,128)(2,1)S(1)} %collective-permute-done.3.refs_1_, bf16[768,256]{1,0:T(8,128)(2,1)S(1)} %collective-permute-done.12.refs_2_, ...), custom_call_target="tpu_custom_call" | custom-call | flops 268435456 | bytes 3145728 | tf_op jit(solution)/shard_map/chain_last/pallas_call | solution.py:312
  94.2 3.1 %collective-permute-start.23 = (bf16[256,256]{1,0:T(8,128)(2,1)S(1)}, bf16[256,256]{1,0:T(8,128)(2,1)S(1)}, u32[]{:S(2)}, u32[]{:S(2)}) collective-permute-start(bf16[256,256]{1,0:T(8,128)(2,1)S(1)} %get-tuple-element.68), channel_id=1, source_target_pairs={{0,40},{8,224},{16,56},{24,240},{32,72},{40,0},{48,88},{56,16},{64... | collective-permute-start | bytes 393224 | tf_op jit(solution)/shard_map/ppermute | solution.py:24
  98.7 2.7 %collective-permute-done.23 = bf16[256,256]{1,0:T(8,128)(2,1)S(1)} collective-permute-done((bf16[256,256]{1,0:T(8,128)(2,1)S(1)}, bf16[256,256]{1,0:T(8,128)(2,1)S(1)}, u32[]{:S(2)}, u32[]{:S(2)}) %collective-permute-start.23) | collective-permute-done | bytes 131104 | tf_op jit(solution)/shard_map/ppermute | solution.py:24
  (74 shorter events, 22.9 us)
Async XLA Ops:
  4.9 34.1 %collective-permute-start.4 = (bf16[2816,256]{1,0:T(8,128)(2,1)}, bf16[2816,256]{1,0:T(8,128)(2,1)S(1)}, u32[]{:S(2)}, u32[]{:S(2)}) collective-permute-start(bf16[2816,256]{1,0:T(8,128)(2,1)} %get-tuple-element.44), channel_id=1, source_target_pairs={{0,16},{8,24},{16,0},{24,8},{32,48},{40,56},{48,32},{56,40},{64,80... | collective-permute-start | bytes 4325384 | tf_op jit(solution)/shard_map/ppermute | solution.py:18
  7.1 31.9 %collective-permute-start.3 = (bf16[2048,256]{1,0:T(8,128)(2,1)}, bf16[2048,256]{1,0:T(8,128)(2,1)S(1)}, u32[]{:S(2)}, u32[]{:S(2)}) collective-permute-start(bf16[2048,256]{1,0:T(8,128)(2,1)} %get-tuple-element.43), channel_id=1, source_target_pairs={{0,8},{8,0},{16,24},{24,16},{32,40},{40,32},{48,56},{56,48},{64,72... | collective-permute-start | bytes 3145736 | tf_op jit(solution)/shard_map/ppermute | solution.py:18
  17.0 9.0 %collective-permute-start = (bf16[2,128,512]{2,1,0:T(8,128)(2,1)S(1)}, bf16[2,128,512]{2,1,0:T(8,128)(2,1)S(1)}, u32[]{:S(2)}, u32[]{:S(2)}) collective-permute-start(bf16[2,128,512]{2,1,0:T(8,128)(2,1)S(1)} %get-tuple-element.41), channel_id=1, source_target_pairs={{0,2},{1,3},{2,4},{3,5},{4,6},{5,7},{6,0},{7,1},{8,10},{9,11},{10,... | collective-permute-start | bytes 786440 | tf_op jit(solution)/shard_map/ppermute | solution.py:31
  18.3 9.4 %collective-permute-start.6 = (bf16[2,128,512]{2,1,0:T(8,128)(2,1)S(1)}, bf16[2,128,512]{2,1,0:T(8,128)(2,1)S(1)}, u32[]{:S(2)}, u32[]{:S(2)}) collective-permute-start(bf16[2,128,512]{2,1,0:T(8,128)(2,1)S(1)} %get-tuple-element.51), channel_id=1, source_target_pairs={{0,6},{1,7},{2,0},{3,1},{4,2},{5,3},{6,4},{7,5},{8,14},{9,15},{10,... | collective-permute-start | bytes 786440 | tf_op jit(solution)/shard_map/ppermute | solution.py:31
  19.8 11.9 %collective-permute-start.2 = (bf16[2,128,512]{2,1,0:T(8,128)(2,1)S(1)}, bf16[2,128,512]{2,1,0:T(8,128)(2,1)S(1)}, u32[]{:S(2)}, u32[]{:S(2)}) collective-permute-start(bf16[2,128,512]{2,1,0:T(8,128)(2,1)S(1)} %get-tuple-element.42), channel_id=1, source_target_pairs={{0,2},{1,3},{2,4},{3,5},{4,6},{5,7},{6,0},{7,1},{8,10},{9,11},{10,... | collective-permute-start | bytes 786440 | tf_op jit(solution)/shard_map/ppermute | solution.py:31
  26.0 13.0 %collective-permute-start.5 = (bf16[2,128,512]{2,1,0:T(8,128)(2,1)S(1)}, bf16[2,128,512]{2,1,0:T(8,128)(2,1)S(1)}, u32[]{:S(2)}, u32[]{:S(2)}) collective-permute-start(bf16[2,128,512]{2,1,0:T(8,128)(2,1)S(1)} %get-tuple-element.49), channel_id=1, source_target_pairs={{0,6},{1,7},{2,0},{3,1},{4,2},{5,3},{6,4},{7,5},{8,14},{9,15},{10,... | collective-permute-start | bytes 786440 | tf_op jit(solution)/shard_map/ppermute | solution.py:31
  27.7 11.4 %collective-permute-start.1 = (bf16[2,128,512]{2,1,0:T(8,128)(2,1)S(1)}, bf16[2,128,512]{2,1,0:T(8,128)(2,1)S(1)}, u32[]{:S(2)}, u32[]{:S(2)}) collective-permute-start(bf16[2,128,512]{2,1,0:T(8,128)(2,1)S(1)} %add_convert_fusion.1), channel_id=1, source_target_pairs={{0,2},{1,3},{2,4},{3,5},{4,6},{5,7},{6,0},{7,1},{8,10},{9,11},{10,... | collective-permute-start | bytes 786440 | tf_op jit(solution)/shard_map/ppermute | solution.py:31
  31.7 7.4 %collective-permute-start.7 = (bf16[2,128,512]{2,1,0:T(8,128)(2,1)S(1)}, bf16[2,128,512]{2,1,0:T(8,128)(2,1)S(1)}, u32[]{:S(2)}, u32[]{:S(2)}) collective-permute-start(bf16[2,128,512]{2,1,0:T(8,128)(2,1)S(1)} %add_convert_fusion), channel_id=1, source_target_pairs={{0,6},{1,7},{2,0},{3,1},{4,2},{5,3},{6,4},{7,5},{8,14},{9,15},{10,... | collective-permute-start | bytes 786440 | tf_op jit(solution)/shard_map/ppermute | solution.py:31
  39.3 6.6 %collective-permute-start.9 = (bf16[256,512]{1,0:T(8,128)(2,1)S(1)}, bf16[256,512]{1,0:T(8,128)(2,1)S(1)}, u32[]{:S(2)}, u32[]{:S(2)}) collective-permute-start(bf16[256,512]{1,0:T(8,128)(2,1)S(1)} %get-tuple-element.54), channel_id=1, source_target_pairs={{0,16},{8,24},{16,0},{24,8},{32,48},{40,56},{48,32},{56,40},{64,80... | collective-permute-start | bytes 786440 | tf_op jit(solution)/shard_map/ppermute | solution.py:18
  39.9 7.0 %collective-permute-start.10 = (bf16[256,512]{1,0:T(8,128)(2,1)S(1)}, bf16[256,512]{1,0:T(8,128)(2,1)S(1)}, u32[]{:S(2)}, u32[]{:S(2)}) collective-permute-start(bf16[256,512]{1,0:T(8,128)(2,1)S(1)} %get-tuple-element.53), channel_id=1, source_target_pairs={{0,17},{1,16},{2,19},{3,18},{4,21},{5,20},{6,23},{7,22},{8,25},{9,... | collective-permute-start | bytes 786440 | tf_op jit(solution)/shard_map/ppermute | solution.py:36
  42.3 10.9 %collective-permute-start.8 = (bf16[256,512]{1,0:T(8,128)(2,1)S(1)}, bf16[256,512]{1,0:T(8,128)(2,1)S(1)}, u32[]{:S(2)}, u32[]{:S(2)}) collective-permute-start(bf16[256,512]{1,0:T(8,128)(2,1)S(1)} %get-tuple-element.53), channel_id=1, source_target_pairs={{0,1},{1,0},{2,3},{3,2},{4,5},{5,4},{6,7},{7,6},{8,9},{9,8},{10,11... | collective-permute-start | bytes 786440 | tf_op jit(solution)/shard_map/ppermute | solution.py:31
  42.8 15.5 %collective-permute-start.14 = (bf16[1280,256]{1,0:T(8,128)(2,1)S(1)}, bf16[1280,256]{1,0:T(8,128)(2,1)S(1)}, u32[]{:S(2)}, u32[]{:S(2)}) collective-permute-start(bf16[1280,256]{1,0:T(8,128)(2,1)S(1)} %slice.14), channel_id=1, source_target_pairs={{0,8},{8,0},{16,24},{24,16},{32,40},{40,32},{48,56},{56,48},{64,72... | collective-permute-start | bytes 1966088 | tf_op jit(solution)/shard_map/ppermute | solution.py:18
  54.2 4.1 %collective-permute-start.11 = (bf16[512,512]{1,0:T(8,128)(2,1)S(1)}, bf16[512,512]{1,0:T(8,128)(2,1)S(1)}, u32[]{:S(2)}, u32[]{:S(2)}) collective-permute-start(bf16[512,512]{1,0:T(8,128)(2,1)S(1)} %get-tuple-element.59.refs_4_.refs_6_), channel_id=1, source_target_pairs={{0,8},{8,0},{16,24},{24,16},{32,40},{40,32},{48,56},{56,48},{64,72... | collective-permute-start | bytes 1572872 | tf_op jit(solution)/shard_map/ppermute | solution.py:18
  59.6 12.7 %collective-permute-start.15 = (bf16[512,256]{1,0:T(8,128)(2,1)}, bf16[512,256]{1,0:T(8,128)(2,1)}, u32[]{:S(2)}, u32[]{:S(2)}) collective-permute-start(bf16[512,256]{1,0:T(8,128)(2,1)} %chain_start.3), channel_id=1, source_target_pairs={{0,32},{8,232},{16,48},{24,248},{32,64},{40,8},{48,80},{56,24},{64... | collective-permute-start | bytes 786440 | tf_op jit(solution)/shard_map/ppermute | solution.py:24
  66.2 7.6 %collective-permute-start.16 = (bf16[256,512]{1,0:T(8,128)(2,1)}, bf16[256,512]{1,0:T(8,128)(2,1)}, u32[]{:S(2)}, u32[]{:S(2)}) collective-permute-start(bf16[256,512]{1,0:T(8,128)(2,1)} %chain_start.4), channel_id=1, source_target_pairs={{0,64},{8,200},{16,80},{24,216},{32,96},{40,232},{48,112},{56,248}... | collective-permute-start | bytes 786440 | tf_op jit(solution)/shard_map/ppermute | solution.py:24
  68.8 13.0 %collective-permute-start.20 = (bf16[512,256]{1,0:T(8,128)(2,1)}, bf16[512,256]{1,0:T(8,128)(2,1)}, u32[]{:S(2)}, u32[]{:S(2)}) collective-permute-start(bf16[512,256]{1,0:T(8,128)(2,1)} %chain_start.5), channel_id=1, source_target_pairs={{0,32},{8,232},{16,48},{24,248},{32,64},{40,8},{48,80},{56,24},{64... | collective-permute-start | bytes 786440 | tf_op jit(solution)/shard_map/ppermute | solution.py:24
  69.5 14.0 %collective-permute-start.12 = (bf16[768,256]{1,0:T(8,128)(2,1)}, bf16[768,256]{1,0:T(8,128)(2,1)S(1)}, u32[]{:S(2)}, u32[]{:S(2)}) collective-permute-start(bf16[768,256]{1,0:T(8,128)(2,1)} %get-tuple-element.62), channel_id=1, source_target_pairs={{0,16},{8,24},{16,0},{24,8},{32,48},{40,56},{48,32},{56,40},{64,80... | collective-permute-start | bytes 1179656 | tf_op jit(solution)/shard_map/ppermute | solution.py:18
  69.5 19.7 %collective-permute-start.13 = (bf16[768,256]{1,0:T(8,128)(2,1)}, bf16[768,256]{1,0:T(8,128)(2,1)}, u32[]{:S(2)}, u32[]{:S(2)}) collective-permute-start(bf16[768,256]{1,0:T(8,128)(2,1)} %get-tuple-element.63), channel_id=1, source_target_pairs={{0,24},{8,16},{16,8},{24,0},{32,56},{40,48},{48,40},{56,32},{64,88... | collective-permute-start | bytes 1179656 | tf_op jit(solution)/shard_map/ppermute | solution.py:18
  78.0 11.3 %collective-permute-start.17 = (bf16[512,256]{1,0:T(8,128)(2,1)S(1)}, bf16[512,256]{1,0:T(8,128)(2,1)S(1)}, u32[]{:S(2)}, u32[]{:S(2)}) collective-permute-start(bf16[512,256]{1,0:T(8,128)(2,1)S(1)} %chain_middle.2), channel_id=1, source_target_pairs={{0,32},{8,232},{16,48},{24,248},{32,64},{40,8},{48,80},{56,24},{64... | collective-permute-start | bytes 786440 | tf_op jit(solution)/shard_map/ppermute | solution.py:24
  83.4 9.2 %collective-permute-start.21 = (bf16[512,256]{1,0:T(8,128)(2,1)S(1)}, bf16[512,256]{1,0:T(8,128)(2,1)S(1)}, u32[]{:S(2)}, u32[]{:S(2)}) collective-permute-start(bf16[512,256]{1,0:T(8,128)(2,1)S(1)} %chain_middle.3), channel_id=1, source_target_pairs={{0,32},{8,232},{16,48},{24,248},{32,64},{40,8},{48,80},{56,24},{64... | collective-permute-start | bytes 786440 | tf_op jit(solution)/shard_map/ppermute | solution.py:24
  90.9 7.8 %collective-permute-start.18 = (bf16[256,256]{1,0:T(8,128)(2,1)S(1)}, bf16[256,256]{1,0:T(8,128)(2,1)S(1)}, u32[]{:S(2)}, u32[]{:S(2)}) collective-permute-start(bf16[256,256]{1,0:T(8,128)(2,1)S(1)} %get-tuple-element.65), channel_id=1, source_target_pairs={{0,32},{8,232},{16,48},{24,248},{32,64},{40,8},{48,80},{56,24},{64... | collective-permute-start | bytes 393224 | tf_op jit(solution)/shard_map/ppermute | solution.py:24
  91.0 7.7 %collective-permute-start.19 = (bf16[256,256]{1,0:T(8,128)(2,1)S(1)}, bf16[256,256]{1,0:T(8,128)(2,1)S(1)}, u32[]{:S(2)}, u32[]{:S(2)}) collective-permute-start(bf16[256,256]{1,0:T(8,128)(2,1)S(1)} %get-tuple-element.66), channel_id=1, source_target_pairs={{0,40},{8,224},{16,56},{24,240},{32,72},{40,0},{48,88},{56,16},{64... | collective-permute-start | bytes 393224 | tf_op jit(solution)/shard_map/ppermute | solution.py:24
  94.1 4.6 %collective-permute-start.22 = (bf16[256,256]{1,0:T(8,128)(2,1)S(1)}, bf16[256,256]{1,0:T(8,128)(2,1)S(1)}, u32[]{:S(2)}, u32[]{:S(2)}) collective-permute-start(bf16[256,256]{1,0:T(8,128)(2,1)S(1)} %get-tuple-element.67), channel_id=1, source_target_pairs={{0,32},{8,232},{16,48},{24,248},{32,64},{40,8},{48,80},{56,24},{64... | collective-permute-start | bytes 393224 | tf_op jit(solution)/shard_map/ppermute | solution.py:24
  94.2 7.1 %collective-permute-start.23 = (bf16[256,256]{1,0:T(8,128)(2,1)S(1)}, bf16[256,256]{1,0:T(8,128)(2,1)S(1)}, u32[]{:S(2)}, u32[]{:S(2)}) collective-permute-start(bf16[256,256]{1,0:T(8,128)(2,1)S(1)} %get-tuple-element.68), channel_id=1, source_target_pairs={{0,40},{8,224},{16,56},{24,240},{32,72},{40,0},{48,88},{56,16},{64... | collective-permute-start | bytes 393224 | tf_op jit(solution)/shard_map/ppermute | solution.py:24
  (15 other events, 158.4 us)

commit v3 on v2

--- a/solution.py
+++ b/solution.py
@@ -10,7 +10,7 @@
 BF = jnp.bfloat16
 F32 = jnp.float32
 CHUNKS = 2
-SPLIT = 5
+SPLIT = 6
 
 
 def swap(x, bits):
@@ -137,18 +137,7 @@
     )(own, from0, from1, back0, back1, z_sep)
 
 
-def block_of(me, m, j):
-    peer = me ^ m
-    z, pair, side = peer >> 2, (peer >> 1) & 1, peer & 1
-    sign = 1 - 2 * side
-    if j == 0:
-        z, side = z + 4, side
-    elif j < 7:
-        z, side = z + sign * (3 - (j - 1) // 2), (j - 1) % 2
-    return ((z + 8) & 7) * 4 + pair * 2 + side
-
-
-def pick_kernel(wanted, place, mask, factor, extra, *refs):
+def pick_kernel(wanted, table, mask, factor, *refs):
     outs = refs[: len(wanted)]
     held, in_sem, out_sem = refs[len(wanted) :]
     jobs = []
@@ -157,59 +146,42 @@
         jobs += [(o, m, j, at) for at, (m, j) in enumerate(order)]
     reads, writes = [], []
     for i, (o, m, j, at) in enumerate(jobs):
-        block = pl.multiple_of(block_of(place[0], m, j) * 256, 256)
+        block = pl.multiple_of(table[m * 8 + j] * 256, 256)
         reads.append(pltpu.make_async_copy(factor.at[pl.ds(block, 256), :], held.at[i], in_sem.at[i]))
-        reads[-1].start()
-    if extra is not None:
-        tail = outs[-1].shape[0] - 256
-        reads.append(pltpu.make_async_copy(extra, held.at[len(jobs)], in_sem.at[len(jobs)]))
         reads[-1].start()
     for i, (o, m, j, at) in enumerate(jobs):
         reads[i].wait()
-        keep = mask[block_of(place[0], m, j)].astype(F32)
+        keep = mask[table[m * 8 + j]].astype(F32)
         held[i] = (held[i].astype(F32) * keep).astype(BF)
         writes.append(
             pltpu.make_async_copy(held.at[i], outs[o].at[pl.ds(at * 256, 256), :], out_sem.at[i])
         )
         writes[-1].start()
-    if extra is not None:
-        reads[-1].wait()
-        writes.append(
-            pltpu.make_async_copy(held.at[len(jobs)], outs[-1].at[pl.ds(tail, 256), :], out_sem.at[len(jobs)])
-        )
-        writes[-1].start()
     for copy in writes:
         copy.wait()
 
 
-def pick(place, mask, factor, wanted, limit, extra=None):
+def pick(factor, table, mask, wanted):
     sizes = [sum(hi - lo for _, lo, hi in groups) for groups in wanted]
     total = sum(sizes)
-    kernel = functools.partial(pick_kernel, wanted)
-    args = [factor]
-    if extra is None:
-        kernel = lambda place, mask, factor, *refs: pick_kernel(wanted, place, mask, factor, None, *refs)
-    else:
-        sizes[-1] += 1
-        args.append(extra)
-    return pl.pallas_call(
-        kernel,
+    return pl.pallas_call(
+        functools.partial(pick_kernel, wanted),
         grid_spec=pltpu.PrefetchScalarGridSpec(
             num_scalar_prefetch=2,
             grid=(1,),
-            in_specs=[pl.BlockSpec(memory_space=pl.ANY)] * len(args),
+            in_specs=[pl.BlockSpec(memory_space=pl.ANY)],
             out_specs=[pl.BlockSpec(memory_space=pl.ANY)] * len(wanted),
             scratch_shapes=[
-                pltpu.VMEM((total + 1, 256, 256), BF),
-                pltpu.SemaphoreType.DMA((total + 1,)),
-                pltpu.SemaphoreType.DMA((total + 1,)),
+                pltpu.VMEM((total, 256, 256), BF),
+                pltpu.SemaphoreType.DMA((total,)),
+                pltpu.SemaphoreType.DMA((total,)),
             ],
         ),
         out_shape=[jax.ShapeDtypeStruct((size * 256, 256), BF) for size in sizes],
-        compiler_params=pltpu.CompilerParams(vmem_limit_bytes=limit),
+        compiler_params=pltpu.CompilerParams(vmem_limit_bytes=60 << 20),
         cost_estimate=pl.CostEstimate(flops=total << 16, bytes_accessed=total << 18, transcendentals=0),
         name="pick_factor",
-    )(place, mask, *args)
+    )(table, mask, factor)
 
 
 def sep_kernel(rest_ref, part_ref, near_ref, cross_ref, inv_ref, near_inv_ref, y_ref, pair_ref):
@@ -218,22 +190,13 @@
     y_ref[...] = y
     near = (near_ref[...].astype(F32) - cross_ref[...].astype(F32)).astype(BF)
     pair_ref[0:256, :] = y
-    pair_ref[256:512, :] = jnp.dot(near_inv_ref[...], near, preferred_element_type=F32).astype(BF)
-
-
-def sep_solve(rest, part, near, cross, sep_inverse, far_f):
+    pair_ref[256:512, :] = jnp.dot(near_inv_ref[0], near, preferred_element_type=F32).astype(BF)
+
+
+def sep_solve(rest, part, near, cross, sep_inverse, near_inverse):
     rows, samples = rest.shape
-    whole = pl.BlockSpec((rows, samples), lambda i: (0, 0))
-    last = far_f.shape[0] // rows - 1
     return pl.pallas_call(
         sep_kernel,
-        grid=(1,),
-        in_specs=[whole] * 4
-        + [
-            pl.BlockSpec((1, rows, rows), lambda i: (0, 0, 0)),
-            pl.BlockSpec((rows, rows), lambda i: (last, 0)),
-        ],
-        out_specs=[whole, pl.BlockSpec((2 * rows, samples), lambda i: (0, 0))],
         out_shape=[
             jax.ShapeDtypeStruct((rows, samples), BF),
             jax.ShapeDtypeStruct((2 * rows, samples), BF),
@@ -241,7 +204,7 @@
         compiler_params=pltpu.CompilerParams(vmem_limit_bytes=16 << 20),
         cost_estimate=pl.CostEstimate(flops=140_000_000, bytes_accessed=2 << 20, transcendentals=0),
         name="sep_solve",
-    )(rest, part, near, cross, sep_inverse, far_f)
+    )(rest, part, near, cross, sep_inverse, near_inverse)
 
 
 def multiply(f, y):
@@ -314,9 +277,9 @@
         grid_spec=pltpu.PrefetchScalarGridSpec(
             num_scalar_prefetch=1,
             grid=(2,),
-            in_specs=[pl.BlockSpec((256, 256), lambda i, c, k=k: (k + (c[0] ^ i), 0)) for k in first]
+            in_specs=[pl.BlockSpec((256, 256), lambda i, c, k=k: (k + (c[0] + i) % 2, 0)) for k in first]
             + [pl.BlockSpec((256, width), lambda i, c, m=m: (m // 2, chunk)) for m in range(4)]
-            + [pl.BlockSpec((256, width), lambda i, c: (c[0] ^ i, 0))],
+            + [pl.BlockSpec((256, width), lambda i, c: ((c[0] + i) % 2, 0))],
             out_specs=[pl.BlockSpec((256, width), lambda i, c: (0, 0))] * 2,
         ),
         out_shape=[jax.ShapeDtypeStruct((256, width), BF)] * 2,
@@ -361,29 +324,49 @@
     columns = lax.axis_size("col")
     samples = z_sep.shape[1]
     me = lax.axis_index("row").astype(jnp.int32)
+    core = me % 2
+    table = []
+    for m in range(4):
+        peer = me ^ m
+        sign = 1 - 2 * (peer % 2)
+        base = me // 4
+        pair = (peer // 2) % 2
+        side = peer % 2
+
+        def block(z, k):
+            return ((z + 16) % 8) * 4 + pair * 2 + k
+
+        table.append(block(base + 4, side))
+        for d in (3, 2):
+            for k in (0, 1):
+                table.append(block(base + d * sign, k))
+        table.append(block(base, side))
+        for k in (0, 1):
+            table.append(block(base + sign, k))
+    table = jnp.stack(table).astype(jnp.int32)
+    mask = reader_mask[0, 0]
+
     col = lax.axis_index("col").astype(jnp.int32)
-    core = me & 1
-    place = jnp.stack([me, col >> 1, col & 1])
-    mask = reader_mask[0, 0]
-
+    where = jnp.stack([me, col >> 1, col & 1])
     near_f, far_a = pick(
-        place, mask, top_factor[0], (((1, 0, 8),), ((2, 0, SPLIT), (3, 0, SPLIT))), 60 << 20, sep_inverse[0]
-    )
+        top_factor[0], table, mask, (((1, 0, 8),), ((2, 0, SPLIT), (3, 0, SPLIT)))
+    )
+    near_inverse = swap(sep_inverse, 2)
+    z_leaf, near_f, far_a, near_inverse = lax.optimization_barrier((z_leaf, near_f, far_a, near_inverse))
     far_a = swap(far_a, 2)
-    z_leaf, near_f = lax.optimization_barrier((z_leaf, near_f))
     near_f = swap(near_f, 1)
     y_leaf, up2, down2, up0, up1, down0, down1, own = leaf_solve(
-        place, z_leaf, leaf_inverse, lower_separator_coupling, leaf_parent, leaf_offset, 2 * columns
+        where, z_leaf, leaf_inverse, lower_separator_coupling, leaf_parent, leaf_offset, 2 * columns
     )
     from2, back2 = across(up2, 1), across(down2, 3)
     from1, back0 = across(up1, 1), across(down0, 3)
     own_f, far_b, cross_b = pick(
-        place, mask, top_factor[0], (((0, 0, 8),), ((2, SPLIT, 8),), ((3, SPLIT, 8),)), 16 << 20)
-    from1, near_f, far_a, own_f, far_b, cross_b = lax.optimization_barrier(
-        (from1, near_f, far_a, own_f, far_b, cross_b)
-    )
-    cross_a = swap(far_a[SPLIT * 256 : 2 * SPLIT * 256], 1)
-    near_inverse = far_a[2 * SPLIT * 256 :]
+        top_factor[0], table, mask, (((0, 0, 8),), ((2, SPLIT, 8),), ((3, SPLIT, 8),))
+    )
+    from1, near_f, far_a, own_f, far_b, cross_b, near_inverse = lax.optimization_barrier(
+        (from1, near_f, far_a, own_f, far_b, cross_b, near_inverse)
+    )
+    cross_a = swap(far_a[SPLIT * 256 :], 1)
     from0 = across((up0.astype(F32) + from2.astype(F32)).astype(BF), 1)
     back1 = across((down1.astype(F32) + back2.astype(F32)).astype(BF), 3)
     part, mine, rest = gather_x(own, from0, from1, back0, back1, z_sep)
@@ -392,21 +375,21 @@
     pair_core = swap(pair, 1)
     pair_core, far_b, cross_b = lax.optimization_barrier((pair_core, far_b, cross_b))
     far_b, cross_b = swap(far_b, 2), swap(cross_b, 3)
+    first_f = [own_f, near_f, far_a, cross_a]
+    last_f = [own_f, near_f, far_b, cross_b]
+    skip = (SPLIT, SPLIT, 0, 0)
     panels = [pair, pair_core, pair, pair_core]
-    first_f = [own_f, near_f, far_a, cross_a]
-    skip = (SPLIT, SPLIT, 0, 0)
 
     core_id = core.reshape(1)
     width = samples // CHUNKS
     far = chain(start(first_f, 0, 1, panels, 0, samples), 2)
     arrived = [chain(start(first_f, 1, 2, panels, c, width)) for c in range(CHUNKS)]
-    sums = [middle(core_id, first_f, 3, panels, c, width, arrived[c], far) for c in range(CHUNKS)]
-    last_f = [own_f, near_f, far_b, cross_b]
-    arrived = [chain(x) for x in sums]
+    for c in range(CHUNKS):
+        arrived[c] = chain(middle(core_id, first_f, 3, panels, c, width, arrived[c], far))
     for c in range(CHUNKS):
         same, other = last(core_id, last_f, skip, panels, c, width, arrived[c])
         arrived[c] = (chain(same), chain(other, 1, 1))
-    rest = own_rows(last_f, [k + 2 for k in skip], panels, z_top[0])
+    rest = own_rows(first_f, [5] * 4, panels, z_top[0])
     tops = [
         rest[:, c * width : (c + 1) * width] - (arrived[c][0].astype(F32) + arrived[c][1].astype(F32))
         for c in range(CHUNKS)

time: 103 us -> 102 us (level)
  Pallas kernels: 29.2 us -> 21.9 us
  starting transfers between devices: 36.7 us -> 41.3 us
  local copies, waits for them, and re-layouts: 4.17 us -> 6.66 us
    ppermute x7 -> x8, waiting for transfers between devices: 7.97 us -> 4.04 us  [swap(): return lax.ppermute(x, 'row', [(i, i ^ bits) for i in range(n)])]
    ppermute x7 -> x8, starting transfers between devices: 11.9 us -> 15.2 us  [swap(): return lax.ppermute(x, 'row', [(i, i ^ bits) for i in range(n)])]
    ppermute x9, starting transfers between devices: 16.1 us -> 19.2 us  [chain(): lax.ppermute(x, 'row', [(i, (i + (hop if i % 2 == 0 else n - hop)) % n ^...]
    pallas_call x3, Pallas kernels: 10.4 us -> 7.83 us  [the longest x2 6.88 us: pick(): pl.pallas_call(functools.partial(pick_kernel, wanted), grid_spec=pltpu.Pr...]
    ppermute x9, waiting for transfers between devices: 4.24 us -> 6.45 us  [chain(): lax.ppermute(x, 'row', [(i, (i + (hop if i % 2 == 0 else n - hop)) % n ^...]
    pallas_call x3, Pallas kernels: 3.82 us -> 1.79 us  [start(): pl.pallas_call(start_kernel, grid=(blocks,), in_specs=[pl.BlockSpec((256,...]
    pallas_call x2, Pallas kernels: 3.29 us -> 1.4 us  [middle(): pl.pallas_call(middle_kernel, grid_spec=pltpu.PrefetchScalarGridSpec(num_...]
    unnamed x30 -> x34, local copies, waits for them, and re-layouts: 4.12 us -> 5.94 us
  transfers between devices with their start and end apart: 24 -> 25, of which waited for: 9 -> 12; matrix products, arithmetic and copies ran while one was open for 0% -> 2% of each run, Pallas kernels for 23% -> 19%
where the time goes in v3:
time: 102 us
  starting transfers between devices  41.3 us (40%)
  waiting for transfers between devices  28.7 us (28%)
  Pallas kernels  21.9 us (21%)
  local copies, waits for them, and re-layouts  6.66 us (7%)
  other arithmetic  2.58 us (3%)
    ppermute x9, starting transfers between devices, chain(): lax.ppermute(x, 'row', [(i, (i + (hop if i % 2 == 0 else n - hop)) % n ^...  19.2 us
    ppermute x7, waiting for transfers between devices, across(): lax.ppermute(x, 'col', [(i, (i + 2 * step) % n ^ cross) for i in range(n)])  17.3 us
    ppermute x8, starting transfers between devices, swap(): return lax.ppermute(x, 'row', [(i, i ^ bits) for i in range(n)])  15.2 us
    pallas_call x1, Pallas kernels, leaf_solve(): pl.pallas_call(leaf_kernel, grid_spec=pltpu.PrefetchScalarGridSpec(num_sc...  7.66 us
    pallas_call x2, Pallas kernels, pick(): pl.pallas_call(functools.partial(pick_kernel, wanted), grid_spec=pltpu.Pr...  6.88 us
    ppermute x9, waiting for transfers between devices, chain(): lax.ppermute(x, 'row', [(i, (i + (hop if i % 2 == 0 else n - hop)) % n ^...  6.45 us
    unnamed x34, local copies, waits for them, and re-layouts  5.94 us
    ppermute x7, starting transfers between devices, across(): lax.ppermute(x, 'col', [(i, (i + 2 * step) % n ^ cross) for i in range(n)])  5.31 us
  transfers between devices with their start and end apart: 25, of which 12 were waited for; matrix products, arithmetic and copies ran while one was open for 2% of the time, Pallas kernels for 19%

profile of v3, /device:TPU:1, one launch (start us, length us, event | category | flops | bytes accessed | tf_op | source)
XLA Modules:
  0.0 101.9 jit_solution(7637553600327144456)
XLA Ops:
  0.6 2.2 %collective-permute-start = (bf16[1,256,256]{2,1,0:T(8,128)(2,1)}, bf16[1,256,256]{2,1,0:T(8,128)(2,1)S(1)}, u32[]{:S(2)}, u32[]{:S(2)}) collective-permute-start(bf16[1,256,256]{2,1,0:T(8,128)(2,1)} %inv_ref.3), channel_id=1, source_target_pairs={{0,16},{8,24},{16,0},{24,8},{32,48},{40,56},{48,32},{56,40},{64,80... | collective-permute-start | bytes 393224 | tf_op jit(solution)/shard_map/ppermute | solution.py:18
  3.5 3.7 %pick_factor.2 = (bf16[2048,256]{1,0:T(8,128)(2,1)}, bf16[3072,256]{1,0:T(8,128)(2,1)}) custom-call(s32[32]{0:T(128)} %stack.147.table, s32[32]{0:T(128)} %bitcast.44, bf16[8192,256]{1,0:T(8,128)(2,1)} %bitcast.42), custom_call_target="tpu_custom_call" | custom-call | flops 1310720 | bytes 5242880 | tf_op jit(solution)/shard_map/pick_factor/pallas_call | solution.py:167
  8.5 2.6 %collective-permute-start.4 = (bf16[2048,256]{1,0:T(8,128)(2,1)}, bf16[2048,256]{1,0:T(8,128)(2,1)S(1)}, u32[]{:S(2)}, u32[]{:S(2)}) collective-permute-start(bf16[2048,256]{1,0:T(8,128)(2,1)} %get-tuple-element.47), channel_id=1, source_target_pairs={{0,8},{8,0},{16,24},{24,16},{32,40},{40,32},{48,56},{56,48},{64,72... | collective-permute-start | bytes 3145736 | tf_op jit(solution)/shard_map/ppermute | solution.py:18
  11.1 1.6 %copy-done.1 = bf16[2048,512]{1,0:T(8,128)(2,1)S(1)} copy-done((bf16[2048,512]{1,0:T(8,128)(2,1)S(1)}, bf16[2048,512]{1,0:T(8,128)(2,1)}, u32[]{:S(2)}) %copy-start.1) | copy-done | bytes 2097176
  13.8 7.7 %leaf_solve.1 = (bf16[2048,512]{1,0:T(8,128)(2,1)}, bf16[2,128,512]{2,1,0:T(8,128)(2,1)S(1)}, bf16[2,128,512]{2,1,0:T(8,128)(2,1)S(1)}, bf16[2,128,512]{2,1,0:T(...) custom-call(s32[3]{0:T(128)S(1)} %pad_add_fusion.place, ...), custom_call_target="tpu_custom_call" | custom-call | flops 810000000 | bytes 8388608 | tf_op jit(solution)/shard_map/leaf_solve/pallas_call | solution.py:88
  22.5 2.6 %collective-permute-start.7 = (bf16[2,128,512]{2,1,0:T(8,128)(2,1)S(1)}, bf16[2,128,512]{2,1,0:T(8,128)(2,1)S(1)}, u32[]{:S(2)}, u32[]{:S(2)}) collective-permute-start(bf16[2,128,512]{2,1,0:T(8,128)(2,1)S(1)} %get-tuple-element.56), channel_id=1, source_target_pairs={{0,6},{1,7},{2,0},{3,1},{4,2},{5,3},{6,4},{7,5},{8,14},{9,15},{10,... | collective-permute-start | bytes 786440 | tf_op jit(solution)/shard_map/ppermute | solution.py:31
  25.1 6.4 %collective-permute-done.1 = bf16[2,128,512]{2,1,0:T(8,128)(2,1)S(1)} collective-permute-done((bf16[2,128,512]{2,1,0:T(8,128)(2,1)S(1)}, bf16[2,128,512]{2,1,0:T(8,128)(2,1)S(1)}, u32[]{:S(2)}, u32[]{:S(2)}) %collective-permute-start.1) | collective-permute-done | bytes 262176 | tf_op jit(solution)/shard_map/ppermute | solution.py:31
  34.5 2.6 %collective-permute-done.3.from1 = bf16[2,128,512]{2,1,0:T(8,128)(2,1)S(1)} collective-permute-done((bf16[2,128,512]{2,1,0:T(8,128)(2,1)S(1)}, bf16[2,128,512]{2,1,0:T(8,128)(2,1)S(1)}, u32[]{:S(2)}, u32[]{:S(2)}) %collective-permute-start.3) | collective-permute-done | bytes 262176 | tf_op jit(solution)/shard_map/ppermute | solution.py:31
  38.0 3.2 %pick_factor.3 = (bf16[2048,256]{1,0:T(8,128)(2,1)}, bf16[512,256]{1,0:T(8,128)(2,1)}, bf16[512,256]{1,0:T(8,128)(2,1)}) custom-call(s32[32]{0:T(128)} %stack.147.table, s32[32]{0:T(128)} %bitcast.45, bf16[8192,256]{1,0:T(8,128)(2,1)} %bitcast.43), custom_call_target="tpu_custom_call" | custom-call | flops 786432 | bytes 3145728 | tf_op jit(solution)/shard_map/pick_factor/pallas_call | solution.py:167
  42.2 2.5 %collective-permute-done.8.back1 = bf16[2,128,512]{2,1,0:T(8,128)(2,1)} collective-permute-done((bf16[2,128,512]{2,1,0:T(8,128)(2,1)}, bf16[2,128,512]{2,1,0:T(8,128)(2,1)}, u32[]{:S(2)}, u32[]{:S(2)}) %collective-permute-start.8) | collective-permute-done | bytes 262176 | tf_op jit(solution)/shard_map/ppermute | solution.py:31
  47.7 1.6 %collective-permute-start.11 = (bf16[256,512]{1,0:T(8,128)(2,1)S(1)}, bf16[256,512]{1,0:T(8,128)(2,1)S(1)}, u32[]{:S(2)}, u32[]{:S(2)}) collective-permute-start(bf16[256,512]{1,0:T(8,128)(2,1)S(1)} %get-tuple-element.58), channel_id=1, source_target_pairs={{0,17},{1,16},{2,19},{3,18},{4,21},{5,20},{6,23},{7,22},{8,25},{9,... | collective-permute-start | bytes 786440 | tf_op jit(solution)/shard_map/ppermute | solution.py:36
  50.4 3.1 %collective-permute-start.12 = (bf16[1536,256]{1,0:T(8,128)(2,1)S(1)}, bf16[1536,256]{1,0:T(8,128)(2,1)S(1)}, u32[]{:S(2)}, u32[]{:S(2)}) collective-permute-start(bf16[1536,256]{1,0:T(8,128)(2,1)S(1)} %slice.9), channel_id=1, source_target_pairs={{0,8},{8,0},{16,24},{24,16},{32,40},{40,32},{48,56},{56,48},{64,72... | collective-permute-start | bytes 2359304 | tf_op jit(solution)/shard_map/ppermute | solution.py:18
  54.3 5.8 %collective-permute-done.9.part_ref = bf16[256,512]{1,0:T(8,128)(2,1)S(1)} collective-permute-done((bf16[256,512]{1,0:T(8,128)(2,1)S(1)}, bf16[256,512]{1,0:T(8,128)(2,1)S(1)}, u32[]{:S(2)}, u32[]{:S(2)}) %collective-permute-start.9) | collective-permute-done | bytes 262176 | tf_op jit(solution)/shard_map/ppermute | solution.py:31
  61.1 3.2 %collective-permute-start.13 = (bf16[512,512]{1,0:T(8,128)(2,1)S(1)}, bf16[512,512]{1,0:T(8,128)(2,1)S(1)}, u32[]{:S(2)}, u32[]{:S(2)}) collective-permute-start(bf16[512,512]{1,0:T(8,128)(2,1)S(1)} %get-tuple-element.65.refs_4_.refs_6_), channel_id=1, source_target_pairs={{0,8},{8,0},{16,24},{24,16},{32,40},{40,32},{48,56},{56,48},{64,72... | collective-permute-start | bytes 1572872 | tf_op jit(solution)/shard_map/ppermute | solution.py:18
  66.5 5.0 %collective-permute-start.16 = (bf16[512,256]{1,0:T(8,128)(2,1)S(1)}, bf16[512,256]{1,0:T(8,128)(2,1)S(1)}, u32[]{:S(2)}, u32[]{:S(2)}) collective-permute-start(bf16[512,256]{1,0:T(8,128)(2,1)S(1)} %chain_start.3), channel_id=1, source_target_pairs={{0,32},{8,232},{16,48},{24,248},{32,64},{40,8},{48,80},{56,24},{64... | collective-permute-start | bytes 786440 | tf_op jit(solution)/shard_map/ppermute | solution.py:24
  74.9 2.7 %collective-permute-start.15 = (bf16[512,256]{1,0:T(8,128)(2,1)S(1)}, bf16[512,256]{1,0:T(8,128)(2,1)S(1)}, u32[]{:S(2)}, u32[]{:S(2)}) collective-permute-start(bf16[512,256]{1,0:T(8,128)(2,1)S(1)} %copy-done.15), channel_id=1, source_target_pairs={{0,24},{8,16},{16,8},{24,0},{32,56},{40,48},{48,40},{56,32},{64,88... | collective-permute-start | bytes 786440 | tf_op jit(solution)/shard_map/ppermute | solution.py:18
  77.6 2.8 %collective-permute-done.17.refs_9_ = bf16[256,512]{1,0:T(8,128)(2,1)S(1)} collective-permute-done((bf16[256,512]{1,0:T(8,128)(2,1)S(1)}, bf16[256,512]{1,0:T(8,128)(2,1)S(1)}, u32[]{:S(2)}, u32[]{:S(2)}) %collective-permute-start.17) | collective-permute-done | bytes 262176 | tf_op jit(solution)/shard_map/ppermute | solution.py:24
  81.1 2.7 %collective-permute-start.18 = (bf16[512,256]{1,0:T(8,128)(2,1)S(1)}, bf16[512,256]{1,0:T(8,128)(2,1)S(1)}, u32[]{:S(2)}, u32[]{:S(2)}) collective-permute-start(bf16[512,256]{1,0:T(8,128)(2,1)S(1)} %chain_middle.2), channel_id=1, source_target_pairs={{0,32},{8,232},{16,48},{24,248},{32,64},{40,8},{48,80},{56,24},{64... | collective-permute-start | bytes 786440 | tf_op jit(solution)/shard_map/ppermute | solution.py:24
  84.6 2.6 %collective-permute-start.22 = (bf16[512,256]{1,0:T(8,128)(2,1)S(1)}, bf16[512,256]{1,0:T(8,128)(2,1)S(1)}, u32[]{:S(2)}, u32[]{:S(2)}) collective-permute-start(bf16[512,256]{1,0:T(8,128)(2,1)S(1)} %chain_middle.3), channel_id=1, source_target_pairs={{0,32},{8,232},{16,48},{24,248},{32,64},{40,8},{48,80},{56,24},{64... | collective-permute-start | bytes 786440 | tf_op jit(solution)/shard_map/ppermute | solution.py:24
  87.1 1.5 %collective-permute-done.15.refs_3_ = bf16[512,256]{1,0:T(8,128)(2,1)S(1)} collective-permute-done((bf16[512,256]{1,0:T(8,128)(2,1)S(1)}, bf16[512,256]{1,0:T(8,128)(2,1)S(1)}, u32[]{:S(2)}, u32[]{:S(2)}) %collective-permute-start.15) | collective-permute-done | bytes 262176 | tf_op jit(solution)/shard_map/ppermute | solution.py:18
  89.4 1.7 %collective-permute-start.19 = (bf16[256,256]{1,0:T(8,128)(2,1)S(1)}, bf16[256,256]{1,0:T(8,128)(2,1)S(1)}, u32[]{:S(2)}, u32[]{:S(2)}) collective-permute-start(bf16[256,256]{1,0:T(8,128)(2,1)S(1)} %get-tuple-element.71), channel_id=1, source_target_pairs={{0,32},{8,232},{16,48},{24,248},{32,64},{40,8},{48,80},{56,24},{64... | collective-permute-start | bytes 393224 | tf_op jit(solution)/shard_map/ppermute | solution.py:24
  91.1 2.5 %collective-permute-start.20 = (bf16[256,256]{1,0:T(8,128)(2,1)S(1)}, bf16[256,256]{1,0:T(8,128)(2,1)S(1)}, u32[]{:S(2)}, u32[]{:S(2)}) collective-permute-start(bf16[256,256]{1,0:T(8,128)(2,1)S(1)} %get-tuple-element.72), channel_id=1, source_target_pairs={{0,40},{8,224},{16,56},{24,240},{32,72},{40,0},{48,88},{56,16},{64... | collective-permute-start | bytes 393224 | tf_op jit(solution)/shard_map/ppermute | solution.py:24
  94.8 2.1 %collective-permute-start.24 = (bf16[256,256]{1,0:T(8,128)(2,1)S(1)}, bf16[256,256]{1,0:T(8,128)(2,1)S(1)}, u32[]{:S(2)}, u32[]{:S(2)}) collective-permute-start(bf16[256,256]{1,0:T(8,128)(2,1)S(1)} %get-tuple-element.74), channel_id=1, source_target_pairs={{0,40},{8,224},{16,56},{24,240},{32,72},{40,0},{48,88},{56,16},{64... | collective-permute-start | bytes 393224 | tf_op jit(solution)/shard_map/ppermute | solution.py:24
  98.1 2.8 %collective-permute-done.24 = bf16[256,256]{1,0:T(8,128)(2,1)S(1)} collective-permute-done((bf16[256,256]{1,0:T(8,128)(2,1)S(1)}, bf16[256,256]{1,0:T(8,128)(2,1)S(1)}, u32[]{:S(2)}, u32[]{:S(2)}) %collective-permute-start.24) | collective-permute-done | bytes 131104 | tf_op jit(solution)/shard_map/ppermute | solution.py:24
  (80 shorter events, 25.9 us)
Async XLA Ops:
  0.6 6.6 %collective-permute-start = (bf16[1,256,256]{2,1,0:T(8,128)(2,1)}, bf16[1,256,256]{2,1,0:T(8,128)(2,1)S(1)}, u32[]{:S(2)}, u32[]{:S(2)}) collective-permute-start(bf16[1,256,256]{2,1,0:T(8,128)(2,1)} %inv_ref.3), channel_id=1, source_target_pairs={{0,16},{8,24},{16,0},{24,8},{32,48},{40,56},{48,32},{56,40},{64,80... | collective-permute-start | bytes 393224 | tf_op jit(solution)/shard_map/ppermute | solution.py:18
  7.9 34.3 %collective-permute-start.5 = (bf16[3072,256]{1,0:T(8,128)(2,1)}, bf16[3072,256]{1,0:T(8,128)(2,1)S(1)}, u32[]{:S(2)}, u32[]{:S(2)}) collective-permute-start(bf16[3072,256]{1,0:T(8,128)(2,1)} %get-tuple-element.48), channel_id=1, source_target_pairs={{0,16},{8,24},{16,0},{24,8},{32,48},{40,56},{48,32},{56,40},{64,80... | collective-permute-start | bytes 4718600 | tf_op jit(solution)/shard_map/ppermute | solution.py:18
  8.5 32.7 %collective-permute-start.4 = (bf16[2048,256]{1,0:T(8,128)(2,1)}, bf16[2048,256]{1,0:T(8,128)(2,1)S(1)}, u32[]{:S(2)}, u32[]{:S(2)}) collective-permute-start(bf16[2048,256]{1,0:T(8,128)(2,1)} %get-tuple-element.47), channel_id=1, source_target_pairs={{0,8},{8,0},{16,24},{24,16},{32,40},{40,32},{48,56},{56,48},{64,72... | collective-permute-start | bytes 3145736 | tf_op jit(solution)/shard_map/ppermute | solution.py:18
  22.4 9.1 %collective-permute-start.1 = (bf16[2,128,512]{2,1,0:T(8,128)(2,1)S(1)}, bf16[2,128,512]{2,1,0:T(8,128)(2,1)S(1)}, u32[]{:S(2)}, u32[]{:S(2)}) collective-permute-start(bf16[2,128,512]{2,1,0:T(8,128)(2,1)S(1)} %get-tuple-element.45), channel_id=1, source_target_pairs={{0,2},{1,3},{2,4},{3,5},{4,6},{5,7},{6,0},{7,1},{8,10},{9,11},{10,... | collective-permute-start | bytes 786440 | tf_op jit(solution)/shard_map/ppermute | solution.py:31
  22.5 9.9 %collective-permute-start.7 = (bf16[2,128,512]{2,1,0:T(8,128)(2,1)S(1)}, bf16[2,128,512]{2,1,0:T(8,128)(2,1)S(1)}, u32[]{:S(2)}, u32[]{:S(2)}) collective-permute-start(bf16[2,128,512]{2,1,0:T(8,128)(2,1)S(1)} %get-tuple-element.56), channel_id=1, source_target_pairs={{0,6},{1,7},{2,0},{3,1},{4,2},{5,3},{6,4},{7,5},{8,14},{9,15},{10,... | collective-permute-start | bytes 786440 | tf_op jit(solution)/shard_map/ppermute | solution.py:31
  25.1 12.0 %collective-permute-start.3 = (bf16[2,128,512]{2,1,0:T(8,128)(2,1)S(1)}, bf16[2,128,512]{2,1,0:T(8,128)(2,1)S(1)}, u32[]{:S(2)}, u32[]{:S(2)}) collective-permute-start(bf16[2,128,512]{2,1,0:T(8,128)(2,1)S(1)} %get-tuple-element.46), channel_id=1, source_target_pairs={{0,2},{1,3},{2,4},{3,5},{4,6},{5,7},{6,0},{7,1},{8,10},{9,11},{10,... | collective-permute-start | bytes 786440 | tf_op jit(solution)/shard_map/ppermute | solution.py:31
  31.5 10.7 %collective-permute-start.6 = (bf16[2,128,512]{2,1,0:T(8,128)(2,1)}, bf16[2,128,512]{2,1,0:T(8,128)(2,1)}, u32[]{:S(2)}, u32[]{:S(2)}) collective-permute-start(bf16[2,128,512]{2,1,0:T(8,128)(2,1)} %get-tuple-element.54), channel_id=1, source_target_pairs={{0,6},{1,7},{2,0},{3,1},{4,2},{5,3},{6,4},{7,5},{8,14},{9,15},{10,... | collective-permute-start | bytes 786440 | tf_op jit(solution)/shard_map/ppermute | solution.py:31
  32.4 9.7 %collective-permute-start.2 = (bf16[2,128,512]{2,1,0:T(8,128)(2,1)}, bf16[2,128,512]{2,1,0:T(8,128)(2,1)}, u32[]{:S(2)}, u32[]{:S(2)}) collective-permute-start(bf16[2,128,512]{2,1,0:T(8,128)(2,1)} %add_convert_fusion.1), channel_id=1, source_target_pairs={{0,2},{1,3},{2,4},{3,5},{4,6},{5,7},{6,0},{7,1},{8,10},{9,11},{10,... | collective-permute-start | bytes 786440 | tf_op jit(solution)/shard_map/ppermute | solution.py:31
  37.8 6.9 %collective-permute-start.8 = (bf16[2,128,512]{2,1,0:T(8,128)(2,1)}, bf16[2,128,512]{2,1,0:T(8,128)(2,1)}, u32[]{:S(2)}, u32[]{:S(2)}) collective-permute-start(bf16[2,128,512]{2,1,0:T(8,128)(2,1)} %add_convert_fusion), channel_id=1, source_target_pairs={{0,6},{1,7},{2,0},{3,1},{4,2},{5,3},{6,4},{7,5},{8,14},{9,15},{10,... | collective-permute-start | bytes 786440 | tf_op jit(solution)/shard_map/ppermute | solution.py:31
  47.0 6.5 %collective-permute-start.10 = (bf16[256,512]{1,0:T(8,128)(2,1)S(1)}, bf16[256,512]{1,0:T(8,128)(2,1)S(1)}, u32[]{:S(2)}, u32[]{:S(2)}) collective-permute-start(bf16[256,512]{1,0:T(8,128)(2,1)S(1)} %get-tuple-element.59), channel_id=1, source_target_pairs={{0,16},{8,24},{16,0},{24,8},{32,48},{40,56},{48,32},{56,40},{64,80... | collective-permute-start | bytes 786440 | tf_op jit(solution)/shard_map/ppermute | solution.py:18
  47.7 6.6 %collective-permute-start.11 = (bf16[256,512]{1,0:T(8,128)(2,1)S(1)}, bf16[256,512]{1,0:T(8,128)(2,1)S(1)}, u32[]{:S(2)}, u32[]{:S(2)}) collective-permute-start(bf16[256,512]{1,0:T(8,128)(2,1)S(1)} %get-tuple-element.58), channel_id=1, source_target_pairs={{0,17},{1,16},{2,19},{3,18},{4,21},{5,20},{6,23},{7,22},{8,25},{9,... | collective-permute-start | bytes 786440 | tf_op jit(solution)/shard_map/ppermute | solution.py:36
  49.4 10.8 %collective-permute-start.9 = (bf16[256,512]{1,0:T(8,128)(2,1)S(1)}, bf16[256,512]{1,0:T(8,128)(2,1)S(1)}, u32[]{:S(2)}, u32[]{:S(2)}) collective-permute-start(bf16[256,512]{1,0:T(8,128)(2,1)S(1)} %get-tuple-element.58), channel_id=1, source_target_pairs={{0,1},{1,0},{2,3},{3,2},{4,5},{5,4},{6,7},{7,6},{8,9},{9,8},{10,11... | collective-permute-start | bytes 786440 | tf_op jit(solution)/shard_map/ppermute | solution.py:31
  50.4 15.4 %collective-permute-start.12 = (bf16[1536,256]{1,0:T(8,128)(2,1)S(1)}, bf16[1536,256]{1,0:T(8,128)(2,1)S(1)}, u32[]{:S(2)}, u32[]{:S(2)}) collective-permute-start(bf16[1536,256]{1,0:T(8,128)(2,1)S(1)} %slice.9), channel_id=1, source_target_pairs={{0,8},{8,0},{16,24},{24,16},{32,40},{40,32},{48,56},{56,48},{64,72... | collective-permute-start | bytes 2359304 | tf_op jit(solution)/shard_map/ppermute | solution.py:18
  61.1 4.7 %collective-permute-start.13 = (bf16[512,512]{1,0:T(8,128)(2,1)S(1)}, bf16[512,512]{1,0:T(8,128)(2,1)S(1)}, u32[]{:S(2)}, u32[]{:S(2)}) collective-permute-start(bf16[512,512]{1,0:T(8,128)(2,1)S(1)} %get-tuple-element.65.refs_4_.refs_6_), channel_id=1, source_target_pairs={{0,8},{8,0},{16,24},{24,16},{32,40},{40,32},{48,56},{56,48},{64,72... | collective-permute-start | bytes 1572872 | tf_op jit(solution)/shard_map/ppermute | solution.py:18
  66.5 11.1 %collective-permute-start.16 = (bf16[512,256]{1,0:T(8,128)(2,1)S(1)}, bf16[512,256]{1,0:T(8,128)(2,1)S(1)}, u32[]{:S(2)}, u32[]{:S(2)}) collective-permute-start(bf16[512,256]{1,0:T(8,128)(2,1)S(1)} %chain_start.3), channel_id=1, source_target_pairs={{0,32},{8,232},{16,48},{24,248},{32,64},{40,8},{48,80},{56,24},{64... | collective-permute-start | bytes 786440 | tf_op jit(solution)/shard_map/ppermute | solution.py:24
  71.9 8.5 %collective-permute-start.17 = (bf16[256,512]{1,0:T(8,128)(2,1)S(1)}, bf16[256,512]{1,0:T(8,128)(2,1)S(1)}, u32[]{:S(2)}, u32[]{:S(2)}) collective-permute-start(bf16[256,512]{1,0:T(8,128)(2,1)S(1)} %chain_start.4), channel_id=1, source_target_pairs={{0,64},{8,200},{16,80},{24,216},{32,96},{40,232},{48,112},{56,248}... | collective-permute-start | bytes 786440 | tf_op jit(solution)/shard_map/ppermute | solution.py:24
  73.9 9.9 %collective-permute-start.21 = (bf16[512,256]{1,0:T(8,128)(2,1)S(1)}, bf16[512,256]{1,0:T(8,128)(2,1)S(1)}, u32[]{:S(2)}, u32[]{:S(2)}) collective-permute-start(bf16[512,256]{1,0:T(8,128)(2,1)S(1)} %chain_start.5), channel_id=1, source_target_pairs={{0,32},{8,232},{16,48},{24,248},{32,64},{40,8},{48,80},{56,24},{64... | collective-permute-start | bytes 786440 | tf_op jit(solution)/shard_map/ppermute | solution.py:24
  74.7 12.4 %collective-permute-start.14 = (bf16[512,256]{1,0:T(8,128)(2,1)S(1)}, bf16[512,256]{1,0:T(8,128)(2,1)S(1)}, u32[]{:S(2)}, u32[]{:S(2)}) collective-permute-start(bf16[512,256]{1,0:T(8,128)(2,1)S(1)} %copy-done.16), channel_id=1, source_target_pairs={{0,16},{8,24},{16,0},{24,8},{32,48},{40,56},{48,32},{56,40},{64,80... | collective-permute-start | bytes 786440 | tf_op jit(solution)/shard_map/ppermute | solution.py:18
  74.9 13.8 %collective-permute-start.15 = (bf16[512,256]{1,0:T(8,128)(2,1)S(1)}, bf16[512,256]{1,0:T(8,128)(2,1)S(1)}, u32[]{:S(2)}, u32[]{:S(2)}) collective-permute-start(bf16[512,256]{1,0:T(8,128)(2,1)S(1)} %copy-done.15), channel_id=1, source_target_pairs={{0,24},{8,16},{16,8},{24,0},{32,56},{40,48},{48,40},{56,32},{64,88... | collective-permute-start | bytes 786440 | tf_op jit(solution)/shard_map/ppermute | solution.py:18
  81.1 7.5 %collective-permute-start.18 = (bf16[512,256]{1,0:T(8,128)(2,1)S(1)}, bf16[512,256]{1,0:T(8,128)(2,1)S(1)}, u32[]{:S(2)}, u32[]{:S(2)}) collective-permute-start(bf16[512,256]{1,0:T(8,128)(2,1)S(1)} %chain_middle.2), channel_id=1, source_target_pairs={{0,32},{8,232},{16,48},{24,248},{32,64},{40,8},{48,80},{56,24},{64... | collective-permute-start | bytes 786440 | tf_op jit(solution)/shard_map/ppermute | solution.py:24
  84.6 9.0 %collective-permute-start.22 = (bf16[512,256]{1,0:T(8,128)(2,1)S(1)}, bf16[512,256]{1,0:T(8,128)(2,1)S(1)}, u32[]{:S(2)}, u32[]{:S(2)}) collective-permute-start(bf16[512,256]{1,0:T(8,128)(2,1)S(1)} %chain_middle.3), channel_id=1, source_target_pairs={{0,32},{8,232},{16,48},{24,248},{32,64},{40,8},{48,80},{56,24},{64... | collective-permute-start | bytes 786440 | tf_op jit(solution)/shard_map/ppermute | solution.py:24
  89.4 8.0 %collective-permute-start.19 = (bf16[256,256]{1,0:T(8,128)(2,1)S(1)}, bf16[256,256]{1,0:T(8,128)(2,1)S(1)}, u32[]{:S(2)}, u32[]{:S(2)}) collective-permute-start(bf16[256,256]{1,0:T(8,128)(2,1)S(1)} %get-tuple-element.71), channel_id=1, source_target_pairs={{0,32},{8,232},{16,48},{24,248},{32,64},{40,8},{48,80},{56,24},{64... | collective-permute-start | bytes 393224 | tf_op jit(solution)/shard_map/ppermute | solution.py:24
  91.1 6.5 %collective-permute-start.20 = (bf16[256,256]{1,0:T(8,128)(2,1)S(1)}, bf16[256,256]{1,0:T(8,128)(2,1)S(1)}, u32[]{:S(2)}, u32[]{:S(2)}) collective-permute-start(bf16[256,256]{1,0:T(8,128)(2,1)S(1)} %get-tuple-element.72), channel_id=1, source_target_pairs={{0,40},{8,224},{16,56},{24,240},{32,72},{40,0},{48,88},{56,16},{64... | collective-permute-start | bytes 393224 | tf_op jit(solution)/shard_map/ppermute | solution.py:24
  94.8 6.1 %collective-permute-start.24 = (bf16[256,256]{1,0:T(8,128)(2,1)S(1)}, bf16[256,256]{1,0:T(8,128)(2,1)S(1)}, u32[]{:S(2)}, u32[]{:S(2)}) collective-permute-start(bf16[256,256]{1,0:T(8,128)(2,1)S(1)} %get-tuple-element.74), channel_id=1, source_target_pairs={{0,40},{8,224},{16,56},{24,240},{32,72},{40,0},{48,88},{56,16},{64... | collective-permute-start | bytes 393224 | tf_op jit(solution)/shard_map/ppermute | solution.py:24
  (18 other events, 120.1 us)
